TPU v7x, 32 devices: a whole 2x2x4 slice. The times are simulated.
32 devices in a mesh: row: 16 (over z, y, x), col: 2 (over core).
Axes of the slice: x: 2, y: 2, z: 4, core: 2. Of those that a mesh axis runs over, the one named last changes fastest.
Arguments:
- density: float32 [16384, 16384], P('row', 'col'), as said below
Outputs:
- product: float32 [16384, 16384], P('row', 'col')
- occupation: float32 [1], replicated
Inputs may be any that keep to these rules, and one draw needn't show every extreme that they name: density is symmetric: density[i, j] = density[j, i].
All inputs are finite; a program needn't handle non-finite values.
Results may differ from a plain program's by a relative error of at most 0.000078.
Values sent between devices are 32-bit elements; how exact they have to be, the bound alone decides.
No kernel may reach another device: no remote copies, remote signals or barrier semaphores. Data moves between devices by JAX's collectives and lax.ppermute only.
A program may use at most 128 MiB of HBM per device.

v0:
```python
import math

import jax
import jax.numpy as jnp
from jax import lax
from jax.sharding import PartitionSpec as P

N = 16384
PANEL = 128
STEPS = 2


def broadcast(block, axis, holder):
    block = jnp.where(lax.axis_index(axis) == holder, block, jnp.zeros_like(block))
    return lax.psum(block, axis)


def on_device(density):
    rows_blk, cols_blk = density.shape
    stride = N // STEPS
    row_here = lax.axis_index("row")
    col_here = lax.axis_index("col")
    product = jnp.zeros((rows_blk, cols_blk), jnp.float32)
    for step in range(STEPS):
        start = step * stride
        row_owner = start // rows_blk
        row_offset = start % rows_blk
        col_owner = start // cols_blk
        col_offset = start % cols_blk
        col_piece = density[:, col_offset : col_offset + PANEL]
        col_panel = broadcast(col_piece, "col", col_owner)
        row_piece = density[row_offset : row_offset + PANEL, :]
        row_panel = broadcast(row_piece, "row", row_owner)
        product = product + jnp.dot(
            col_panel,
            row_panel,
            precision=lax.Precision.HIGHEST,
            preferred_element_type=jnp.float32,
        )
    global_rows = row_here * rows_blk + lax.iota(jnp.int32, rows_blk)
    global_cols = col_here * cols_blk + lax.iota(jnp.int32, cols_blk)
    on_diag = global_rows[:, None] == global_cols[None, :]
    local_sum = jnp.sum(jnp.where(on_diag, product, jnp.float32(0.0)))
    total = lax.psum(local_sum, ("row", "col"))
    occupation = jnp.reshape(total / (N * math.sqrt(STEPS * PANEL)), (1,))
    return (product, occupation)


def solution(mesh):
    in_specs = (P("row", "col"),)
    out_specs = (P("row", "col"), P())
    return jax.shard_map(
        on_device, mesh=mesh, in_specs=in_specs, out_specs=out_specs, check_vma=False
    )
```

profile of v0, /device:TPU:1, one launch (start us, length us, event | category | flops | bytes accessed | tf_op | source)
XLA Modules:
  0.0 417.7 jit_solution(13371347775931941748)
XLA Ops:
  7.2 0.0 all-reduce.7.cloned.1.call-start
  7.2 2.1 slice_select_fusion.2
  9.3 0.0 all-reduce.7.cloned.1.call-update
  9.3 0.0 all-reduce.5.cloned.1.call-start
  9.4 6.5 %slice_select_fusion = (f32[128,8192]{1,0:T(8,128)}, f32[128,8192]{1,0:T(8,128)}) fusion(f32[1024,8192]{1,0:T(8,128)} %param.1, pred[]{:T(512)S(6)} %eq.28, pred[]{:T(512)S(6)} %eq.26), kind=kLoop, calls=%fused_computation.2 | loop fusion | flops 2097152 | bytes 12582914 | tf_op jit(solution)/shard_map/jit(_where)/select_n | solution.py:14
  15.9 0.0 all-reduce.5.cloned.1.call-update
  15.9 16.6 %all-reduce.7.cloned.1.call-done = (f32[1024,128]{1,0:T(8,128)}, f32[1024,128]{1,0:T(8,128)}) async-done(((f32[1024,128]{1,0:T(8,128)}, f32[1024,128]{1,0:T(8,128)}), (f32[1024,128]{1,0:T(8,128)}, f32[1024,128]{1,0:T(8,128)})) %all-reduce.7.cloned.1.call-update) | async-done | bytes 1048592 | tf_op jit(solution)/shard_map/psum | solution.py:15
  32.5 266.4 %all-reduce.5.cloned.1.call-done = (f32[128,8192]{1,0:T(8,128)}, f32[128,8192]{1,0:T(8,128)}) async-done(((f32[128,8192]{1,0:T(8,128)}, f32[128,8192]{1,0:T(8,128)}), (f32[128,8192]{1,0:T(8,128)}, f32[128,8192]{1,0:T(8,128)})) %all-reduce.5.cloned.1.call-update) | async-done | bytes 8388624 | tf_op jit(solution)/shard_map/psum | solution.py:15
  298.9 0.0 copy-start
  298.9 0.0 copy-start.1
  298.9 31.7 %fusion = f32[1024,8192]{1,0:T(8,128)} fusion(f32[1024,128]{1,0:T(8,128)} %get-tuple-element.4, f32[128,8192]{1,0:T(8,128)} %get-tuple-element.2), kind=kOutput, calls=%fused_computation.8 | convolution fusion | flops 12884901888 | bytes 38273024 | tf_op jit(solution)/shard_map/dot_general | solution.py:34
  330.6 0.0 copy-done
  330.6 0.0 copy-done.1
  330.6 40.5 %select_reduce_fusion = (f32[]{:T(128)}, f32[1024,8192]{1,0:T(8,128)}) fusion(s32[8192]{0:T(1024)S(1)} %iota_add_fusion, s32[1024]{0:T(1024)S(1)} %iota_add_fusion.1, f32[1024,8192]{1,0:T(8,128)} %fusion, f32[1024,128]{1,0:T(8,128)S(1)} %copy-done.1, f32[128,8192]{1,0:T(8,128)S(1)} %copy-done), kind=kOutput, calls=%fused_computation | convolution fusion | flops 12918456320 | bytes 71864320 | tf_op jit(solution)/shard_map/dot_general | solution.py:34
  371.1 38.1 %psum.39 = f32[]{:T(128)} all-reduce(f32[]{:T(128)} %get-tuple-element.10), channel_id=1, replica_groups=mesh['row'=16,'col'=2] {'row','col'}, use_global_device_ids=true, to_apply=%region_5.6 | all-reduce | flops 1 | bytes 8 | tf_op jit(solution)/shard_map/psum | solution.py:44
  (2 shorter events, 0.0 us)
Async XLA Ops:
  7.2 25.4 %all-reduce.7.cloned.1.call-start = ((), (), s32[]{:S(2)}) async-start(), calls=%async_computation.1 | async-start | bytes 2097152 | tf_op jit(solution)/shard_map/psum | solution.py:15
  9.3 289.6 %all-reduce.5.cloned.1.call-start = ((), (), s32[]{:S(2)}) async-start(), calls=%async_computation | async-start | bytes 16777216 | tf_op jit(solution)/shard_map/psum | solution.py:15
  298.9 31.7 %copy-start = (f32[128,8192]{1,0:T(8,128)S(1)}, f32[128,8192]{1,0:T(8,128)}, u32[]{:S(2)}) copy-start(f32[128,8192]{1,0:T(8,128)} %get-tuple-element.3) | copy-start | bytes 12582916
  298.9 31.7 %copy-start.1 = (f32[1024,128]{1,0:T(8,128)S(1)}, f32[1024,128]{1,0:T(8,128)}, u32[]{:S(2)}) copy-start(f32[1024,128]{1,0:T(8,128)} %get-tuple-element.5) | copy-start | bytes 1572868
Sparse Core Ops, SparseCore 0:
  10.4 22.1 all-reduce.6
  40.4 258.4 all-reduce.4
where the time goes:
time: 420 us; the launch traced here: 418 us
  waiting for transfers between devices  283 us (67%)
  matrix products  72.1 us (17%)
  blocking collectives  38.1 us (9%)
  between operations  15.9 us (4%)
  other arithmetic  8.57 us (2%)
    psum x2, waiting for transfers between devices, broadcast(): return lax.psum(block, axis)  283 us
    dot_general x2, matrix products, on_device(): jnp.dot(col_panel, row_panel, precision=lax.Precision.HIGHEST, preferred_...  72.1 us
    psum x1, blocking collectives, on_device(): total = lax.psum(local_sum, ('row', 'col'))  38.1 us
    select_n x2, other arithmetic, broadcast(): jnp.where(lax.axis_index(axis) == holder, block, jnp.zeros_like(block))  8.56 us
  transfers between devices with their start and end apart: 2, of which 2 were waited for; matrix products, arithmetic and copies ran while one was open for 2% of the time, Pallas kernels for 0%

commit v1 on v0

v1 whole, which is shorter than its diff:
```python
import functools
import math

import jax
import jax.numpy as jnp
from jax import lax
from jax.experimental import pallas as pl
from jax.experimental.pallas import tpu as pltpu
from jax.sharding import PartitionSpec as P

PANEL = 128
STEPS = 2
DEPTH = PANEL * STEPS
BLOCK = 512
BOTH = ("row", "col")


VMEM = pl.BlockSpec(memory_space=pltpu.VMEM)
ANY = pl.BlockSpec(memory_space=pl.ANY)
SLAB = 256


def split(x):
    hi = x.astype(jnp.bfloat16)
    lo = (x - hi.astype(jnp.float32)).astype(jnp.bfloat16)
    return hi, lo


def join(mine, other, core):
    return jnp.concatenate(
        [jnp.where(core == 0, mine, other), jnp.where(core == 0, other, mine)], axis=1
    )


def own_kernel(mine, other, left, total, top, bottom):
    x = join(mine[...], other[...], lax.axis_index("col"))
    hi, lo = split(x)
    left[:, 0:DEPTH] = hi
    left[:, DEPTH : 2 * DEPTH] = lo
    left[:, 2 * DEPTH : 3 * DEPTH] = hi
    top[...] = x[:BLOCK]
    bottom[...] = x[BLOCK:]
    total[...] = jnp.full(total.shape, jnp.sum(x * x), jnp.float32)


def like(rows, cols=DEPTH, dtype=jnp.float32):
    return jax.ShapeDtypeStruct((rows, cols), dtype)


def in_vmem(kernel, out_shape, *arrays):
    return pl.pallas_call(
        kernel,
        out_shape=out_shape,
        in_specs=[VMEM] * len(arrays),
        out_specs=(VMEM,) * len(out_shape),
        compiler_params=pltpu.CompilerParams(vmem_limit_bytes=8 * 2**20),
    )(*arrays)


def own_rows(mine, other):
    b = BLOCK
    shapes = (like(2 * b, 3 * DEPTH, jnp.bfloat16), like(8, 128), like(b), like(b))
    return in_vmem(own_kernel, shapes, mine, other)


def stack_kernel(*refs):
    out, at = refs[-1], 0
    for ref in refs[:-1]:
        out[at : at + ref.shape[0]] = ref[...]
        at += ref.shape[0]


def stack(*arrays):
    return in_vmem(stack_kernel, (like(sum(a.shape[0] for a in arrays), PANEL),), *arrays)[0]


def plane_kernel(mine, other, total_own, token, plane, total):
    del token
    core = lax.axis_index("col")
    total[...] = total_own[...]
    for i in range(plane.shape[0] // BLOCK):
        rows = pl.ds(i * BLOCK, BLOCK)
        x = join(mine[rows, :], other[rows, :], core)
        plane[rows, :] = x
        total[...] += jnp.sum(x * x)


def plane_rows(mine, other, total, token):
    return in_vmem(plane_kernel, (like(mine.shape[0]), like(8, 128)), mine, other, total, token)


def after_kernel(token, *refs):
    refs[len(refs) // 2][...] = jnp.zeros((8, 128), jnp.float32)


def after(token, *arrays):
    count = len(arrays)
    return pl.pallas_call(
        after_kernel,
        out_shape=(like(8, 128), *(like(*a.shape) for a in arrays)),
        in_specs=[VMEM] * (1 + count),
        out_specs=(VMEM,) * (1 + count),
        input_output_aliases={1 + i: 1 + i for i in range(count)},
        compiler_params=pltpu.CompilerParams(vmem_limit_bytes=2**20),
    )(token, *arrays)


def halves_kernel(token, x, y, later, x_same, y_same, x_top, y_bottom):
    later[...] = jnp.zeros_like(later)
    h = x_top.shape[0]
    x_top[...] = x[0:h]
    y_bottom[...] = y[h : 2 * h]


def halves(token, x, y):
    rows, cols = x.shape
    return pl.pallas_call(
        halves_kernel,
        out_shape=(like(8, 128), like(rows, cols), like(rows, cols)) + (like(rows // 2, cols),) * 2,
        in_specs=[VMEM] * 3,
        out_specs=(VMEM,) * 5,
        input_output_aliases={1: 1, 2: 2},
        compiler_params=pltpu.CompilerParams(vmem_limit_bytes=2**20),
    )(token, x, y)


def multiply_kernel(blocks, n_arrays, has_product, has_sum, *refs):
    left, arrays = refs[0], refs[1 : 1 + n_arrays]
    at = 1 + n_arrays + has_product
    if has_sum:
        mine, other = refs[at], refs[at + 1]
        at += 2
    product, token = refs[at], refs[at + 1]
    right, out, place, sems = refs[at + 2 :]
    row, core = lax.axis_index("row"), lax.axis_index("col")
    z, y, x = row // 4, (row // 2) % 2, row % 2
    own_half = core == half(z)

    def load(i, source):
        array, at = source
        hi, lo = split(arrays[array][at * BLOCK : (at + 1) * BLOCK, :])
        to = pl.ds(i * BLOCK, BLOCK)
        right[to, 0:DEPTH] = hi
        right[to, DEPTH : 2 * DEPTH] = hi
        right[to, 2 * DEPTH : 3 * DEPTH] = lo

    for i, (sources, odd, dx, dy, part) in enumerate(blocks):
        if len(sources) == 2:

            @pl.when(own_half)
            def _():
                load(i, sources[0])

            @pl.when(jnp.logical_not(own_half))
            def _():
                load(i, sources[1])

        else:
            load(i, sources[0])
        chunk = (((z + odd) % 2) * 2 + (y ^ dy)) * 2 + (x ^ dx)
        place[i] = (chunk * 2 + part) * BLOCK

    if has_sum:
        token[...] = mine[...] + other[...]
    else:
        token[...] = jnp.zeros_like(token)

    def store(i):
        return pltpu.make_async_copy(
            out.at[i], product.at[:, pl.ds(pl.multiple_of(place[i], BLOCK), BLOCK)], sems.at[i]
        )

    @pl.loop(0, len(blocks))
    def _(i):
        out[i] = lax.dot_general(
            left[...],
            right[pl.ds(pl.multiple_of(i * BLOCK, BLOCK), BLOCK), :],
            (((1,), (1,)), ((), ())),
            preferred_element_type=jnp.float32,
        )
        store(i).start()

    @pl.loop(0, len(blocks))
    def _(i):
        store(i).wait()


def multiply(left, blocks, product, cols, sums=None):
    arrays, listed = [], []
    for sources, *whose in blocks:
        found = []
        for array, place in sources:
            known = [i for i, a in enumerate(arrays) if a is array]
            if not known:
                arrays.append(array)
            found.append((known[0] if known else len(arrays) - 1, place))
        listed.append((found, *whose))
    rows, count = left.shape[0], len(blocks)
    operands, in_specs = [left, *arrays], [VMEM] * (1 + len(arrays))
    aliases = {}
    if product is not None:
        aliases = {len(operands): 0}
        operands.append(product)
        in_specs.append(ANY)
    if sums is not None:
        operands += sums
        in_specs += [VMEM] * 2
    return pl.pallas_call(
        functools.partial(
            multiply_kernel, listed, len(arrays), product is not None, sums is not None
        ),
        out_shape=(
            jax.ShapeDtypeStruct((rows, cols), jnp.float32),
            jax.ShapeDtypeStruct((8, 128), jnp.float32),
        ),
        in_specs=in_specs,
        out_specs=(ANY, VMEM),
        scratch_shapes=[
            pltpu.VMEM((count * BLOCK, 3 * DEPTH), jnp.bfloat16),
            pltpu.VMEM((count, rows, BLOCK), jnp.float32),
            pltpu.SMEM((count,), jnp.int32),
            pltpu.SemaphoreType.DMA((count,)),
        ],
        input_output_aliases=aliases,
        compiler_params=pltpu.CompilerParams(vmem_limit_bytes=20 * 2**20),
        cost_estimate=pl.CostEstimate(
            flops=6 * DEPTH * rows * BLOCK * count,
            bytes_accessed=4 * rows * BLOCK * count,
            transcendentals=0,
        ),
    )(*operands)


def half(z):
    return z // 2


def moves(target):
    pairs = []
    for z in range(4):
        for y in range(2):
            for x in range(2):
                for c in range(2):
                    to = target(x, y, z, c)
                    if to is not None:
                        tx, ty, tz, tc = to
                        here = ((z * 2 + y) * 2 + x) * 2 + c
                        there = (((tz % 4) * 2 + ty) * 2 + tx) * 2 + tc
                        pairs.append((here, there))
    return pairs


CORE = moves(lambda x, y, z, c: (x, y, z, 1 - c))
X = moves(lambda x, y, z, c: (1 - x, y, z, c))
Y = moves(lambda x, y, z, c: (x, 1 - y, z, c))
Z_1 = moves(lambda x, y, z, c: (x, y, z ^ 1, c))
Z_2 = moves(lambda x, y, z, c: (x, y, z ^ 2, c))
X_FAR = moves(lambda x, y, z, c: (1 - x, y, z, c) if c != half(z) else None)
Y_FAR = moves(lambda x, y, z, c: (x, 1 - y, z, c) if c != half(z) else None)
Z_NEAR = moves(lambda x, y, z, c: (x, y, z + 1 if c == 1 else z - 1, half(z)))
Z_FAR = moves(
    lambda x, y, z, c: (x, y, z + 1, c) if c == half((z - 1) % 4) else None
)


def send(a, pairs):
    return lax.ppermute(a, BOTH, pairs)


def on_16x2(density):
    rows, cols = density.shape
    n = 16 * rows
    mul = functools.partial(multiply, cols=cols)

    panel = density[:, 0:PANEL]
    sib = send(panel, CORE)
    raw_x, raw_y = send(panel, X), send(panel, Y)
    left, total, top, bottom = own_rows(panel, sib)
    odd_t, odd_b = send(top, Z_NEAR), send(bottom, Z_NEAR)

    token, raw_x, raw_y, x_top, y_bottom = halves(total, raw_x, raw_y)
    raw_xy, raw_yx = send(x_top, Y), send(y_bottom, X)
    token, odd_t = after(token, odd_t)
    odd_t_x, odd_t_y, far_t = send(odd_t, X), send(odd_t, Y), send(odd_t, Z_FAR)
    token, odd_b = after(token, odd_b)
    odd_b_y, odd_b_x, far_b = send(odd_b, Y), send(odd_b, X), send(odd_b, Z_FAR)
    token, raw_xy, raw_yx = after(token, raw_xy, raw_yx)
    plane = stack(raw_x, raw_y, raw_xy, raw_yx)
    sib_plane = send(plane, CORE)
    token, odd_t_x = after(token, odd_t_x)
    odd_xy = send(odd_t_x, Y)
    product, token = mul(
        left,
        [
            ([(odd_t, 0)], 1, 0, 0, 0),
            ([(odd_b, 0)], 1, 0, 0, 1),
            ([(odd_t_x, 0)], 1, 1, 0, 0),
            ([(odd_t_y, 0)], 1, 0, 1, 0),
        ],
        None,
        sums=(token, token),
    )
    token, far_t = after(token, far_t)
    far_t_x = send(far_t, X_FAR)
    token, far_b = after(token, far_b)
    far_b_y = send(far_b, Y_FAR)
    far_t_y, far_b_x = send(far_t, Y_FAR), send(far_b, X_FAR)
    plane, total = plane_rows(plane, sib_plane, total, token)
    total_1 = send(total, Z_1)
    token, odd_b_y = after(total, odd_b_y)
    odd_yx = send(odd_b_y, X)
    token, total, total_1 = after(token, total, total_1)
    product, total = mul(
        left,
        [
            ([(odd_b_x, 0)], 1, 1, 0, 1),
            ([(odd_b_y, 0)], 1, 0, 1, 1),
            ([(top, 0), (far_t, 0)], 0, 0, 0, 0),
            ([(bottom, 0), (far_b, 0)], 0, 0, 0, 1),
        ],
        product,
        sums=(total, total_1),
    )
    total_2 = send(total, Z_2)
    token, far_t_x = after(total, far_t_x)
    far_xy = send(far_t_x, Y_FAR)
    token, far_b_y = after(token, far_b_y)
    far_yx = send(far_b_y, X_FAR)
    token, total, total_2 = after(token, total, total_2)
    product, total = mul(
        left,
        [
            ([(plane, 0), (far_t_x, 0)], 0, 1, 0, 0),
            ([(plane, 1), (far_b_x, 0)], 0, 1, 0, 1),
            ([(plane, 2), (far_t_y, 0)], 0, 0, 1, 0),
            ([(plane, 3), (far_b_y, 0)], 0, 0, 1, 1),
        ],
        product,
        sums=(total, total_2),
    )
    occupation = total[0, 0] / (n * math.sqrt(DEPTH))
    product, token = mul(
        left,
        [([(odd_xy, 0)], 1, 1, 1, 0), ([(odd_yx, 0)], 1, 1, 1, 1)],
        product,
    )
    product, token = mul(
        left,
        [([(plane, 4), (far_xy, 0)], 0, 1, 1, 0), ([(plane, 5), (far_yx, 0)], 0, 1, 1, 1)],
        product,
    )
    return product, jnp.reshape(occupation, (1,))


def on_any(n, density):
    rows, cols = density.shape
    core = lax.axis_index("col")
    pieces = []
    for step in range(STEPS):
        start = step * (n // STEPS)
        at = start % cols
        piece = density[:, at : at + PANEL]
        pieces.append(jnp.where(core == start // cols, piece, 0.0))
    panel = lax.psum(jnp.concatenate(pieces, axis=1), "col")
    occupation = lax.psum(jnp.sum(panel * panel), "row") / (n * math.sqrt(DEPTH))
    whole = lax.all_gather(panel, "row", tiled=True)
    mine = lax.dynamic_slice_in_dim(whole, core * cols, cols, axis=0)
    product = lax.dot_general(
        panel,
        mine,
        (((1,), (1,)), ((), ())),
        precision=lax.Precision.HIGHEST,
        preferred_element_type=jnp.float32,
    )
    return product, jnp.reshape(occupation, (1,))


def solution(mesh):
    sizes = (mesh.shape["row"], mesh.shape["col"])

    def run(density):
        n = density.shape[0]
        body = functools.partial(on_any, n)
        if sizes == (16, 2) and n == 16 * 2 * BLOCK:
            body = on_16x2
        return jax.shard_map(
            body,
            mesh=mesh,
            in_specs=(P("row", "col"),),
            out_specs=(P("row", "col"), P()),
            check_vma=False,
        )(density)

    return run
```

time: 420 us -> 103 us (0.25)
  the two profiles are of different devices: /device:TPU:1 before, /device:TPU:16 now
where the time goes in v1:
time: 103 us; the launch traced here: 102 us
  starting transfers between devices  37.4 us (36%)
  waiting for transfers between devices  32.1 us (31%)
  Pallas kernels  28.6 us (28%)
  between operations  2.71 us (3%)
  local copies, waits for them, and re-layouts  1.59 us (2%)
    ppermute x24, starting transfers between devices, send(): return lax.ppermute(a, BOTH, pairs)  37.4 us
    ppermute x24, waiting for transfers between devices, send(): return lax.ppermute(a, BOTH, pairs)  32.1 us
    pallas_call x5, Pallas kernels, multiply(): pl.pallas_call(functools.partial(multiply_kernel, listed, len(arrays), pr...  25.7 us
  transfers between devices with their start and end apart: 24, of which 7 were waited for; matrix products, arithmetic and copies ran while one was open for 1% of the time, Pallas kernels for 24%

profile of v1, /device:TPU:16, one launch (start us, length us, event | category | flops | bytes accessed | tf_op | source)
XLA Modules:
  0.0 102.3 jit_solution(715287082131514384)
XLA Ops:
  0.6 1.1 %slice.6.mine = f32[1024,128]{1,0:T(8,128)S(1)} slice(f32[1024,8192]{1,0:T(8,128)} %param.1), slice={[0:1024], [0:128]} | slice | bytes 1048576 | tf_op jit(solution)/shard_map/slice | solution.py:275
  1.7 0.1 collective-permute-start
  1.8 1.6 %collective-permute-start.2 = (f32[1024,128]{1,0:T(8,128)S(1)}, f32[1024,128]{1,0:T(8,128)S(1)}, u32[]{:S(2)}, u32[]{:S(2)}) collective-permute-start(f32[1024,128]{1,0:T(8,128)S(1)} %slice.6.mine), channel_id=1, source_target_pairs={{0,4},{1,5},{2,6},{3,7},{4,0},{5,1},{6,2},{7,3},{8,12},{9,13},{10,... | collective-permute-start | bytes 1572872 | tf_op jit(solution)/shard_map/ppermute | solution.py:267
  3.4 1.5 %collective-permute-start.1 = (f32[1024,128]{1,0:T(8,128)S(1)}, f32[1024,128]{1,0:T(8,128)S(1)}, u32[]{:S(2)}, u32[]{:S(2)}) collective-permute-start(f32[1024,128]{1,0:T(8,128)S(1)} %slice.6.mine), channel_id=1, source_target_pairs={{0,2},{1,3},{2,0},{3,1},{4,6},{5,7},{6,4},{7,5},{8,10},{9,11},{10,... | collective-permute-start | bytes 1572872 | tf_op jit(solution)/shard_map/ppermute | solution.py:267
  4.9 0.0 collective-permute-done.other
  4.9 0.8 shard_map.30
  5.7 0.1 collective-permute-start.3
  5.8 1.7 %collective-permute-start.4 = (f32[512,256]{1,0:T(8,128)S(1)}, f32[512,256]{1,0:T(8,128)S(1)}, u32[]{:S(2)}, u32[]{:S(2)}) collective-permute-start(f32[512,256]{1,0:T(8,128)S(1)} %get-tuple-element.51.refs_5_), channel_id=1, source_target_pairs={{0,24},{1,8},{2,26},{3,10},{4,28},{5,12},{6,30},{7,14},{8,0},{9,16... | collective-permute-start | bytes 1572872 | tf_op jit(solution)/shard_map/ppermute | solution.py:267
  7.5 8.6 %collective-permute-done.2.y = f32[1024,128]{1,0:T(8,128)S(1)} collective-permute-done((f32[1024,128]{1,0:T(8,128)S(1)}, f32[1024,128]{1,0:T(8,128)S(1)}, u32[]{:S(2)}, u32[]{:S(2)}) %collective-permute-start.2) | collective-permute-done | bytes 524320 | tf_op jit(solution)/shard_map/ppermute | solution.py:267
  16.1 1.2 %collective-permute-done.1.x = f32[1024,128]{1,0:T(8,128)S(1)} collective-permute-done((f32[1024,128]{1,0:T(8,128)S(1)}, f32[1024,128]{1,0:T(8,128)S(1)}, u32[]{:S(2)}, u32[]{:S(2)}) %collective-permute-start.1) | collective-permute-done | bytes 524320 | tf_op jit(solution)/shard_map/ppermute | solution.py:267
  17.4 0.6 collective-permute-start.5
  18.0 1.5 %collective-permute-start.6 = (f32[512,128]{1,0:T(8,128)S(1)}, f32[512,128]{1,0:T(8,128)S(1)}, u32[]{:S(2)}, u32[]{:S(2)}) collective-permute-start(f32[512,128]{1,0:T(8,128)S(1)} %get-tuple-element.54), channel_id=1, source_target_pairs={{0,2},{1,3},{2,0},{3,1},{4,6},{5,7},{6,4},{7,5},{8,10},{9,11},{10,... | collective-permute-start | bytes 786440 | tf_op jit(solution)/shard_map/ppermute | solution.py:267
  19.5 0.0 collective-permute-done.3.refs_0_
  19.5 11.8 %collective-permute-done.4.refs_0_ = f32[512,256]{1,0:T(8,128)S(1)} collective-permute-done((f32[512,256]{1,0:T(8,128)S(1)}, f32[512,256]{1,0:T(8,128)S(1)}, u32[]{:S(2)}, u32[]{:S(2)}) %collective-permute-start.4) | collective-permute-done | bytes 524320 | tf_op jit(solution)/shard_map/ppermute | solution.py:267
  31.2 0.0 collective-permute-done.5.refs_0_
  31.3 0.1 shard_map.35.mine
  31.4 0.1 collective-permute-start.7
  31.4 0.6 collective-permute-start.8
  32.0 1.3 %collective-permute-start.9 = (f32[512,256]{1,0:T(8,128)S(1)}, f32[512,256]{1,0:T(8,128)S(1)}, u32[]{:S(2)}, u32[]{:S(2)}) collective-permute-start(f32[512,256]{1,0:T(8,128)S(1)} %get-tuple-element.57.refs_1_), channel_id=1, source_target_pairs={{0,4},{1,5},{2,6},{3,7},{4,0},{5,1},{6,2},{7,3},{8,12},{9,13},{10,... | collective-permute-start | bytes 1572872 | tf_op jit(solution)/shard_map/ppermute | solution.py:267
  33.3 3.4 %collective-permute-start.10 = (f32[512,256]{1,0:T(8,128)S(1)}, f32[512,256]{1,0:T(8,128)S(1)}, u32[]{:S(2)}, u32[]{:S(2)}) collective-permute-start(f32[512,256]{1,0:T(8,128)S(1)} %get-tuple-element.57.refs_1_), channel_id=1, source_target_pairs={{1,9},{3,11},{5,13},{7,15},{8,16},{10,18},{12,20},{14,22},{16,24},... | collective-permute-start | bytes 1572872 | tf_op jit(solution)/shard_map/ppermute | solution.py:267
  36.7 1.9 %collective-permute-start.11 = (f32[512,256]{1,0:T(8,128)S(1)}, f32[512,256]{1,0:T(8,128)S(1)}, u32[]{:S(2)}, u32[]{:S(2)}) collective-permute-start(f32[512,256]{1,0:T(8,128)S(1)} %get-tuple-element.58.refs_2_), channel_id=1, source_target_pairs={{1,9},{3,11},{5,13},{7,15},{8,16},{10,18},{12,20},{14,22},{16,24},... | collective-permute-start | bytes 1572872 | tf_op jit(solution)/shard_map/ppermute | solution.py:267
  38.6 7.2 %collective-permute-done.8.refs_0_ = f32[512,256]{1,0:T(8,128)S(1)} collective-permute-done((f32[512,256]{1,0:T(8,128)S(1)}, f32[512,256]{1,0:T(8,128)S(1)}, u32[]{:S(2)}, u32[]{:S(2)}) %collective-permute-start.8) | collective-permute-done | bytes 524320 | tf_op jit(solution)/shard_map/ppermute | solution.py:267
  45.8 0.5 collective-permute-start.13
  46.3 0.0 collective-permute-done.9.refs_4_
  46.3 1.3 %collective-permute-start.12 = (f32[512,256]{1,0:T(8,128)S(1)}, f32[512,256]{1,0:T(8,128)S(1)}, u32[]{:S(2)}, u32[]{:S(2)}) collective-permute-start(f32[512,256]{1,0:T(8,128)S(1)} %get-tuple-element.58.refs_2_), channel_id=1, source_target_pairs={{0,2},{1,3},{2,0},{3,1},{4,6},{5,7},{6,4},{7,5},{8,10},{9,11},{10,... | collective-permute-start | bytes 1572872 | tf_op jit(solution)/shard_map/ppermute | solution.py:267
  47.6 5.8 %shard_map.37 = (f32[1024,8192]{1,0:T(8,128)}, f32[8,128]{1,0:T(8,128)S(1)}) custom-call(bf16[1024,768]{1,0:T(8,128)(2,1)S(1)} %get-tuple-element.44.refs_0_, f32[512,256]{1,0:T(8,128)S(1)} %get-tuple-element.57.refs_1_, f32[512,256]{1,0:T(8,128)S(1)} %get-tuple-element.58.refs_2_, f32[512,256]{1,0:T(8,128)S(1)} %get-tuple-element.60.refs_3_, ...), custom_call_target="tpu_custom_call" | custom-call | flops 3221225472 | bytes 8388608 | tf_op jit(solution)/shard_map/pallas_call | solution.py:208
  53.4 0.0 collective-permute-done.10.refs_0_
  53.5 2.6 %collective-permute-start.17 = (f32[512,256]{1,0:T(8,128)S(1)}, f32[512,256]{1,0:T(8,128)S(1)}, u32[]{:S(2)}, u32[]{:S(2)}) collective-permute-start(f32[512,256]{1,0:T(8,128)S(1)} %get-tuple-element.69.refs_6_), channel_id=1, source_target_pairs={{1,5},{3,7},{5,1},{7,3},{9,13},{11,15},{13,9},{15,11},{16,20},{18,... | collective-permute-start | bytes 1572872 | tf_op jit(solution)/shard_map/ppermute | solution.py:267
  56.1 3.4 %collective-permute-start.15 = (f32[512,256]{1,0:T(8,128)S(1)}, f32[512,256]{1,0:T(8,128)S(1)}, u32[]{:S(2)}, u32[]{:S(2)}) collective-permute-start(f32[512,256]{1,0:T(8,128)S(1)} %get-tuple-element.68.refs_4_), channel_id=1, source_target_pairs={{1,3},{3,1},{5,7},{7,5},{9,11},{11,9},{13,15},{15,13},{16,18},{18,... | collective-permute-start | bytes 1572872 | tf_op jit(solution)/shard_map/ppermute | solution.py:267
  59.5 2.4 %collective-permute-start.21 = (f32[512,256]{1,0:T(8,128)S(1)}, f32[512,256]{1,0:T(8,128)S(1)}, u32[]{:S(2)}, u32[]{:S(2)}) collective-permute-start(f32[512,256]{1,0:T(8,128)S(1)} %get-tuple-element.69.refs_6_), channel_id=1, source_target_pairs={{1,3},{3,1},{5,7},{7,5},{9,11},{11,9},{13,15},{15,13},{16,18},{18,... | collective-permute-start | bytes 1572872 | tf_op jit(solution)/shard_map/ppermute | solution.py:267
  62.0 0.8 shard_map.40
  62.8 1.5 %collective-permute-start.14 = (f32[8,128]{1,0:T(8,128)S(1)}, f32[8,128]{1,0:T(8,128)S(1)}, u32[]{:S(2)}, u32[]{:S(2)}) collective-permute-start(f32[8,128]{1,0:T(8,128)S(1)} %get-tuple-element.66.token.refs_0_), channel_id=1, source_target_pairs={{0,8},{1,9},{2,10},{3,11},{4,12},{5,13},{6,14},{7,15},{8,0},{9,1},... | collective-permute-start | bytes 12296 | tf_op jit(solution)/shard_map/ppermute | solution.py:267
  64.3 2.1 %collective-permute-done.14.refs_1_ = f32[8,128]{1,0:T(8,128)S(1)} collective-permute-done((f32[8,128]{1,0:T(8,128)S(1)}, f32[8,128]{1,0:T(8,128)S(1)}, u32[]{:S(2)}, u32[]{:S(2)}) %collective-permute-start.14) | collective-permute-done | bytes 4128 | tf_op jit(solution)/shard_map/ppermute | solution.py:267
  66.4 3.2 %collective-permute-start.22 = (f32[512,256]{1,0:T(8,128)S(1)}, f32[512,256]{1,0:T(8,128)S(1)}, u32[]{:S(2)}, u32[]{:S(2)}) collective-permute-start(f32[512,256]{1,0:T(8,128)S(1)} %get-tuple-element.68.refs_4_), channel_id=1, source_target_pairs={{1,5},{3,7},{5,1},{7,3},{9,13},{11,15},{13,9},{15,11},{16,20},{18,... | collective-permute-start | bytes 1572872 | tf_op jit(solution)/shard_map/ppermute | solution.py:267
  69.6 0.6 shard_map.42
  70.2 0.7 collective-permute-start.19
  71.0 1.5 %collective-permute-start.20 = (f32[512,256]{1,0:T(8,128)S(1)}, f32[512,256]{1,0:T(8,128)S(1)}, u32[]{:S(2)}, u32[]{:S(2)}) collective-permute-start(f32[512,256]{1,0:T(8,128)S(1)} %get-tuple-element.67.refs_2_), channel_id=1, source_target_pairs={{0,2},{1,3},{2,0},{3,1},{4,6},{5,7},{6,4},{7,5},{8,10},{9,11},{10,... | collective-permute-start | bytes 1572872 | tf_op jit(solution)/shard_map/ppermute | solution.py:267
  72.5 5.8 %shard_map.43 = (f32[1024,8192]{1,0:T(8,128)}, f32[8,128]{1,0:T(8,128)S(1)}) custom-call(bf16[1024,768]{1,0:T(8,128)(2,1)S(1)} %get-tuple-element.44.refs_0_, f32[512,256]{1,0:T(8,128)S(1)} %collective-permute-done.12.refs_1_, f32[512,256]{1,0:T(8,128)S(1)} %get-tuple-element.67.refs_2_, ...), custom_call_target="tpu_custom_call", output_to_operand_aliasing={{0}: (7, {})} | custom-call | flops 3221225472 | bytes 8388608 | tf_op jit(solution)/shard_map/pallas_call | solution.py:208
  78.3 0.1 collective-permute-start.23
  78.4 0.1 collective-permute-done.21.refs_3_
  78.4 3.4 %collective-permute-start.18 = (f32[512,256]{1,0:T(8,128)S(1)}, f32[512,256]{1,0:T(8,128)S(1)}, u32[]{:S(2)}, u32[]{:S(2)}) collective-permute-start(f32[512,256]{1,0:T(8,128)S(1)} %get-tuple-element.77.refs_5_), channel_id=1, source_target_pairs={{1,3},{3,1},{5,7},{7,5},{9,11},{11,9},{13,15},{15,13},{16,18},{18,... | collective-permute-start | bytes 1572872 | tf_op jit(solution)/shard_map/ppermute | solution.py:267
  81.8 1.1 %collective-permute-done.23.refs_1_ = f32[8,128]{1,0:T(8,128)S(1)} collective-permute-done((f32[8,128]{1,0:T(8,128)S(1)}, f32[8,128]{1,0:T(8,128)S(1)}, u32[]{:S(2)}, u32[]{:S(2)}) %collective-permute-start.23) | collective-permute-done | bytes 4128 | tf_op jit(solution)/shard_map/ppermute | solution.py:267
  82.9 2.4 %collective-permute-start.16 = (f32[512,256]{1,0:T(8,128)S(1)}, f32[512,256]{1,0:T(8,128)S(1)}, u32[]{:S(2)}, u32[]{:S(2)}) collective-permute-start(f32[512,256]{1,0:T(8,128)S(1)} %get-tuple-element.75.refs_2_), channel_id=1, source_target_pairs={{1,5},{3,7},{5,1},{7,3},{9,13},{11,15},{13,9},{15,11},{16,20},{18,... | collective-permute-start | bytes 1572872 | tf_op jit(solution)/shard_map/ppermute | solution.py:267
  85.3 0.6 shard_map.46
  85.9 5.8 %shard_map.47 = (f32[1024,8192]{1,0:T(8,128)}, f32[8,128]{1,0:T(8,128)S(1)}) custom-call(bf16[1024,768]{1,0:T(8,128)(2,1)S(1)} %get-tuple-element.44.refs_0_, f32[3072,256]{1,0:T(8,128)S(1)} %get-tuple-element.65.refs_1_, f32[512,256]{1,0:T(8,128)S(1)} %get-tuple-element.75.refs_2_, ...), custom_call_target="tpu_custom_call", output_to_operand_aliasing={{0}: (6, {})} | custom-call | flops 3221225472 | bytes 8388608 | tf_op jit(solution)/shard_map/pallas_call | solution.py:208
  91.7 0.5 slice.7
  92.8 4.1 %shard_map.48 = (f32[1024,8192]{1,0:T(8,128)}, f32[8,128]{1,0:T(8,128)}) custom-call(bf16[1024,768]{1,0:T(8,128)(2,1)S(1)} %get-tuple-element.44.refs_0_, f32[512,256]{1,0:T(8,128)S(1)} %collective-permute-done.19.refs_1_, f32[512,256]{1,0:T(8,128)S(1)} %collective-permute-done.20.refs_2_, ...), custom_call_target="tpu_custom_call", output_to_operand_aliasing={{0}: (3, {})} | custom-call | flops 1610612736 | bytes 4194304 | tf_op jit(solution)/shard_map/pallas_call | solution.py:208
  97.0 4.2 %shard_map.49 = (f32[1024,8192]{1,0:T(8,128)}, f32[8,128]{1,0:T(8,128)}) custom-call(bf16[1024,768]{1,0:T(8,128)(2,1)S(1)} %get-tuple-element.44.refs_0_, f32[3072,256]{1,0:T(8,128)S(1)} %get-tuple-element.65.refs_1_, f32[512,256]{1,0:T(8,128)S(1)} %collective-permute-done.16.refs_2_, ...), custom_call_target="tpu_custom_call", output_to_operand_aliasing={{0}: (4, {})} | custom-call | flops 1610612736 | bytes 4194304 | tf_op jit(solution)/shard_map/pallas_call | solution.py:208
  (22 shorter events, 0.1 us)
Async XLA Ops:
  1.7 3.2 %collective-permute-start = (f32[1024,128]{1,0:T(8,128)S(1)}, f32[1024,128]{1,0:T(8,128)S(1)}, u32[]{:S(2)}, u32[]{:S(2)}) collective-permute-start(f32[1024,128]{1,0:T(8,128)S(1)} %slice.6.mine), channel_id=1, source_target_pairs={{0,1},{1,0},{2,3},{3,2},{4,5},{5,4},{6,7},{7,6},{8,9},{9,8},{10,11... | collective-permute-start | bytes 1572872 | tf_op jit(solution)/shard_map/ppermute | solution.py:267
  1.8 14.3 %collective-permute-start.2 = (f32[1024,128]{1,0:T(8,128)S(1)}, f32[1024,128]{1,0:T(8,128)S(1)}, u32[]{:S(2)}, u32[]{:S(2)}) collective-permute-start(f32[1024,128]{1,0:T(8,128)S(1)} %slice.6.mine), channel_id=1, source_target_pairs={{0,4},{1,5},{2,6},{3,7},{4,0},{5,1},{6,2},{7,3},{8,12},{9,13},{10,... | collective-permute-start | bytes 1572872 | tf_op jit(solution)/shard_map/ppermute | solution.py:267
  3.4 14.0 %collective-permute-start.1 = (f32[1024,128]{1,0:T(8,128)S(1)}, f32[1024,128]{1,0:T(8,128)S(1)}, u32[]{:S(2)}, u32[]{:S(2)}) collective-permute-start(f32[1024,128]{1,0:T(8,128)S(1)} %slice.6.mine), channel_id=1, source_target_pairs={{0,2},{1,3},{2,0},{3,1},{4,6},{5,7},{6,4},{7,5},{8,10},{9,11},{10,... | collective-permute-start | bytes 1572872 | tf_op jit(solution)/shard_map/ppermute | solution.py:267
  5.7 13.8 %collective-permute-start.3 = (f32[512,256]{1,0:T(8,128)S(1)}, f32[512,256]{1,0:T(8,128)S(1)}, u32[]{:S(2)}, u32[]{:S(2)}) collective-permute-start(f32[512,256]{1,0:T(8,128)S(1)} %get-tuple-element.49.refs_3_), channel_id=1, source_target_pairs={{0,24},{1,8},{2,26},{3,10},{4,28},{5,12},{6,30},{7,14},{8,0},{9,16... | collective-permute-start | bytes 1572872 | tf_op jit(solution)/shard_map/ppermute | solution.py:267
  5.8 25.4 %collective-permute-start.4 = (f32[512,256]{1,0:T(8,128)S(1)}, f32[512,256]{1,0:T(8,128)S(1)}, u32[]{:S(2)}, u32[]{:S(2)}) collective-permute-start(f32[512,256]{1,0:T(8,128)S(1)} %get-tuple-element.51.refs_5_), channel_id=1, source_target_pairs={{0,24},{1,8},{2,26},{3,10},{4,28},{5,12},{6,30},{7,14},{8,0},{9,16... | collective-permute-start | bytes 1572872 | tf_op jit(solution)/shard_map/ppermute | solution.py:267
  17.4 13.8 %collective-permute-start.5 = (f32[512,128]{1,0:T(8,128)S(1)}, f32[512,128]{1,0:T(8,128)S(1)}, u32[]{:S(2)}, u32[]{:S(2)}) collective-permute-start(f32[512,128]{1,0:T(8,128)S(1)} %get-tuple-element.53), channel_id=1, source_target_pairs={{0,4},{1,5},{2,6},{3,7},{4,0},{5,1},{6,2},{7,3},{8,12},{9,13},{10,... | collective-permute-start | bytes 786440 | tf_op jit(solution)/shard_map/ppermute | solution.py:267
  18.0 13.3 %collective-permute-start.6 = (f32[512,128]{1,0:T(8,128)S(1)}, f32[512,128]{1,0:T(8,128)S(1)}, u32[]{:S(2)}, u32[]{:S(2)}) collective-permute-start(f32[512,128]{1,0:T(8,128)S(1)} %get-tuple-element.54), channel_id=1, source_target_pairs={{0,2},{1,3},{2,0},{3,1},{4,6},{5,7},{6,4},{7,5},{8,10},{9,11},{10,... | collective-permute-start | bytes 786440 | tf_op jit(solution)/shard_map/ppermute | solution.py:267
  31.4 28.2 %collective-permute-start.7 = (f32[3072,128]{1,0:T(8,128)S(1)}, f32[3072,128]{1,0:T(8,128)S(1)}, u32[]{:S(2)}, u32[]{:S(2)}) collective-permute-start(f32[3072,128]{1,0:T(8,128)S(1)} %shard_map.35.mine), channel_id=1, source_target_pairs={{0,1},{1,0},{2,3},{3,2},{4,5},{5,4},{6,7},{7,6},{8,9},{9,8},{10,11... | collective-permute-start | bytes 4718600 | tf_op jit(solution)/shard_map/ppermute | solution.py:267
  31.4 14.3 %collective-permute-start.8 = (f32[512,256]{1,0:T(8,128)S(1)}, f32[512,256]{1,0:T(8,128)S(1)}, u32[]{:S(2)}, u32[]{:S(2)}) collective-permute-start(f32[512,256]{1,0:T(8,128)S(1)} %get-tuple-element.57.refs_1_), channel_id=1, source_target_pairs={{0,2},{1,3},{2,0},{3,1},{4,6},{5,7},{6,4},{7,5},{8,10},{9,11},{10,... | collective-permute-start | bytes 1572872 | tf_op jit(solution)/shard_map/ppermute | solution.py:267
  32.0 14.3 %collective-permute-start.9 = (f32[512,256]{1,0:T(8,128)S(1)}, f32[512,256]{1,0:T(8,128)S(1)}, u32[]{:S(2)}, u32[]{:S(2)}) collective-permute-start(f32[512,256]{1,0:T(8,128)S(1)} %get-tuple-element.57.refs_1_), channel_id=1, source_target_pairs={{0,4},{1,5},{2,6},{3,7},{4,0},{5,1},{6,2},{7,3},{8,12},{9,13},{10,... | collective-permute-start | bytes 1572872 | tf_op jit(solution)/shard_map/ppermute | solution.py:267
  33.3 20.1 %collective-permute-start.10 = (f32[512,256]{1,0:T(8,128)S(1)}, f32[512,256]{1,0:T(8,128)S(1)}, u32[]{:S(2)}, u32[]{:S(2)}) collective-permute-start(f32[512,256]{1,0:T(8,128)S(1)} %get-tuple-element.57.refs_1_), channel_id=1, source_target_pairs={{1,9},{3,11},{5,13},{7,15},{8,16},{10,18},{12,20},{14,22},{16,24},... | collective-permute-start | bytes 1572872 | tf_op jit(solution)/shard_map/ppermute | solution.py:267
  36.7 16.7 %collective-permute-start.11 = (f32[512,256]{1,0:T(8,128)S(1)}, f32[512,256]{1,0:T(8,128)S(1)}, u32[]{:S(2)}, u32[]{:S(2)}) collective-permute-start(f32[512,256]{1,0:T(8,128)S(1)} %get-tuple-element.58.refs_2_), channel_id=1, source_target_pairs={{1,9},{3,11},{5,13},{7,15},{8,16},{10,18},{12,20},{14,22},{16,24},... | collective-permute-start | bytes 1572872 | tf_op jit(solution)/shard_map/ppermute | solution.py:267
  45.8 17.0 %collective-permute-start.13 = (f32[512,256]{1,0:T(8,128)S(1)}, f32[512,256]{1,0:T(8,128)S(1)}, u32[]{:S(2)}, u32[]{:S(2)}) collective-permute-start(f32[512,256]{1,0:T(8,128)S(1)} %get-tuple-element.58.refs_2_), channel_id=1, source_target_pairs={{0,4},{1,5},{2,6},{3,7},{4,0},{5,1},{6,2},{7,3},{8,12},{9,13},{10,... | collective-permute-start | bytes 1572872 | tf_op jit(solution)/shard_map/ppermute | solution.py:267
  46.3 24.0 %collective-permute-start.12 = (f32[512,256]{1,0:T(8,128)S(1)}, f32[512,256]{1,0:T(8,128)S(1)}, u32[]{:S(2)}, u32[]{:S(2)}) collective-permute-start(f32[512,256]{1,0:T(8,128)S(1)} %get-tuple-element.58.refs_2_), channel_id=1, source_target_pairs={{0,2},{1,3},{2,0},{3,1},{4,6},{5,7},{6,4},{7,5},{8,10},{9,11},{10,... | collective-permute-start | bytes 1572872 | tf_op jit(solution)/shard_map/ppermute | solution.py:267
  53.5 17.5 %collective-permute-start.17 = (f32[512,256]{1,0:T(8,128)S(1)}, f32[512,256]{1,0:T(8,128)S(1)}, u32[]{:S(2)}, u32[]{:S(2)}) collective-permute-start(f32[512,256]{1,0:T(8,128)S(1)} %get-tuple-element.69.refs_6_), channel_id=1, source_target_pairs={{1,5},{3,7},{5,1},{7,3},{9,13},{11,15},{13,9},{15,11},{16,20},{18,... | collective-permute-start | bytes 1572872 | tf_op jit(solution)/shard_map/ppermute | solution.py:267
  56.1 22.1 %collective-permute-start.15 = (f32[512,256]{1,0:T(8,128)S(1)}, f32[512,256]{1,0:T(8,128)S(1)}, u32[]{:S(2)}, u32[]{:S(2)}) collective-permute-start(f32[512,256]{1,0:T(8,128)S(1)} %get-tuple-element.68.refs_4_), channel_id=1, source_target_pairs={{1,3},{3,1},{5,7},{7,5},{9,11},{11,9},{13,15},{15,13},{16,18},{18,... | collective-permute-start | bytes 1572872 | tf_op jit(solution)/shard_map/ppermute | solution.py:267
  59.5 18.9 %collective-permute-start.21 = (f32[512,256]{1,0:T(8,128)S(1)}, f32[512,256]{1,0:T(8,128)S(1)}, u32[]{:S(2)}, u32[]{:S(2)}) collective-permute-start(f32[512,256]{1,0:T(8,128)S(1)} %get-tuple-element.69.refs_6_), channel_id=1, source_target_pairs={{1,3},{3,1},{5,7},{7,5},{9,11},{11,9},{13,15},{15,13},{16,18},{18,... | collective-permute-start | bytes 1572872 | tf_op jit(solution)/shard_map/ppermute | solution.py:267
  62.8 3.7 %collective-permute-start.14 = (f32[8,128]{1,0:T(8,128)S(1)}, f32[8,128]{1,0:T(8,128)S(1)}, u32[]{:S(2)}, u32[]{:S(2)}) collective-permute-start(f32[8,128]{1,0:T(8,128)S(1)} %get-tuple-element.66.token.refs_0_), channel_id=1, source_target_pairs={{0,8},{1,9},{2,10},{3,11},{4,12},{5,13},{6,14},{7,15},{8,0},{9,1},... | collective-permute-start | bytes 12296 | tf_op jit(solution)/shard_map/ppermute | solution.py:267
  66.4 19.5 %collective-permute-start.22 = (f32[512,256]{1,0:T(8,128)S(1)}, f32[512,256]{1,0:T(8,128)S(1)}, u32[]{:S(2)}, u32[]{:S(2)}) collective-permute-start(f32[512,256]{1,0:T(8,128)S(1)} %get-tuple-element.68.refs_4_), channel_id=1, source_target_pairs={{1,5},{3,7},{5,1},{7,3},{9,13},{11,15},{13,9},{15,11},{16,20},{18,... | collective-permute-start | bytes 1572872 | tf_op jit(solution)/shard_map/ppermute | solution.py:267
  70.2 22.6 %collective-permute-start.19 = (f32[512,256]{1,0:T(8,128)S(1)}, f32[512,256]{1,0:T(8,128)S(1)}, u32[]{:S(2)}, u32[]{:S(2)}) collective-permute-start(f32[512,256]{1,0:T(8,128)S(1)} %get-tuple-element.60.refs_3_), channel_id=1, source_target_pairs={{0,4},{1,5},{2,6},{3,7},{4,0},{5,1},{6,2},{7,3},{8,12},{9,13},{10,... | collective-permute-start | bytes 1572872 | tf_op jit(solution)/shard_map/ppermute | solution.py:267
  71.0 21.9 %collective-permute-start.20 = (f32[512,256]{1,0:T(8,128)S(1)}, f32[512,256]{1,0:T(8,128)S(1)}, u32[]{:S(2)}, u32[]{:S(2)}) collective-permute-start(f32[512,256]{1,0:T(8,128)S(1)} %get-tuple-element.67.refs_2_), channel_id=1, source_target_pairs={{0,2},{1,3},{2,0},{3,1},{4,6},{5,7},{6,4},{7,5},{8,10},{9,11},{10,... | collective-permute-start | bytes 1572872 | tf_op jit(solution)/shard_map/ppermute | solution.py:267
  78.3 4.6 %collective-permute-start.23 = (f32[8,128]{1,0:T(8,128)S(1)}, f32[8,128]{1,0:T(8,128)S(1)}, u32[]{:S(2)}, u32[]{:S(2)}) collective-permute-start(f32[8,128]{1,0:T(8,128)S(1)} %get-tuple-element.74.token.refs_0_), channel_id=1, source_target_pairs={{0,16},{1,17},{2,18},{3,19},{4,20},{5,21},{6,22},{7,23},{8,24},{9,... | collective-permute-start | bytes 12296 | tf_op jit(solution)/shard_map/ppermute | solution.py:267
  78.4 18.6 %collective-permute-start.18 = (f32[512,256]{1,0:T(8,128)S(1)}, f32[512,256]{1,0:T(8,128)S(1)}, u32[]{:S(2)}, u32[]{:S(2)}) collective-permute-start(f32[512,256]{1,0:T(8,128)S(1)} %get-tuple-element.77.refs_5_), channel_id=1, source_target_pairs={{1,3},{3,1},{5,7},{7,5},{9,11},{11,9},{13,15},{15,13},{16,18},{18,... | collective-permute-start | bytes 1572872 | tf_op jit(solution)/shard_map/ppermute | solution.py:267
  82.9 14.1 %collective-permute-start.16 = (f32[512,256]{1,0:T(8,128)S(1)}, f32[512,256]{1,0:T(8,128)S(1)}, u32[]{:S(2)}, u32[]{:S(2)}) collective-permute-start(f32[512,256]{1,0:T(8,128)S(1)} %get-tuple-element.75.refs_2_), channel_id=1, source_target_pairs={{1,5},{3,7},{5,1},{7,3},{9,13},{11,15},{13,9},{15,11},{16,20},{18,... | collective-permute-start | bytes 1572872 | tf_op jit(solution)/shard_map/ppermute | solution.py:267

commit v2 on v1

v2 whole, which is shorter than its diff:
```python
import functools
import math

import jax
import jax.numpy as jnp
from jax import lax
from jax.experimental import pallas as pl
from jax.experimental.pallas import tpu as pltpu
from jax.sharding import PartitionSpec as P

PANEL = 128
STEPS = 2
DEPTH = PANEL * STEPS
BLOCK = 512
BOTH = ("row", "col")


VMEM = pl.BlockSpec(memory_space=pltpu.VMEM)
ANY = pl.BlockSpec(memory_space=pl.ANY)
SLAB = 512
LIGHT = pl.CostEstimate(flops=1, bytes_accessed=1, transcendentals=0)
HEAVY = pl.CostEstimate(flops=10**10, bytes_accessed=10**8, transcendentals=0)


def split(x):
    hi = x.astype(jnp.bfloat16)
    lo = (x - hi.astype(jnp.float32)).astype(jnp.bfloat16)
    return hi, lo


def join(mine, other, core):
    return jnp.concatenate(
        [jnp.where(core == 0, mine, other), jnp.where(core == 0, other, mine)], axis=1
    )


def own_kernel(mine, other, left, total, top, bottom, again):
    again[...] = mine[...]
    x = join(mine[...], other[...], lax.axis_index("col"))
    hi, lo = split(x)
    left[:, 0:DEPTH] = hi
    left[:, DEPTH : 2 * DEPTH] = lo
    left[:, 2 * DEPTH : 3 * DEPTH] = hi
    top[...] = x[:BLOCK]
    bottom[...] = x[BLOCK:]
    total[...] = jnp.full(total.shape, jnp.sum(x * x), jnp.float32)


def like(rows, cols=DEPTH, dtype=jnp.float32):
    return jax.ShapeDtypeStruct((rows, cols), dtype)


def in_vmem(kernel, out_shape, *arrays):
    return pl.pallas_call(
        kernel,
        out_shape=out_shape,
        in_specs=[VMEM] * len(arrays),
        out_specs=(VMEM,) * len(out_shape),
        compiler_params=pltpu.CompilerParams(vmem_limit_bytes=8 * 2**20),
        cost_estimate=LIGHT,
    )(*arrays)


def own_rows(mine, other):
    b = BLOCK
    shapes = (like(2 * b, 3 * DEPTH, jnp.bfloat16), like(8, 128), like(b), like(b), like(2 * b, PANEL))
    return in_vmem(own_kernel, shapes, mine, other)


def stack_kernel(*refs):
    out, at = refs[-1], 0
    for ref in refs[:-1]:
        out[at : at + ref.shape[0]] = ref[...]
        at += ref.shape[0]


def stack(*arrays):
    rows, cols = sum(a.shape[0] for a in arrays), arrays[0].shape[1]
    return in_vmem(stack_kernel, (like(rows, cols),), *arrays)[0]


def plane_kernel(mine, other, total_own, token, plane, total):
    del token
    core = lax.axis_index("col")
    rows = plane.shape[0] // 3
    total[...] = total_own[...]
    for i, j in ((0, 1), (1, 0), (2, 2)):
        x = join(mine[i * rows : (i + 1) * rows], other[j * rows : (j + 1) * rows], core)
        plane[i * rows : (i + 1) * rows] = x
        total[...] += jnp.sum(x * x)


def plane_rows(mine, other, total, token):
    return in_vmem(plane_kernel, (like(mine.shape[0]), like(8, 128)), mine, other, total, token)


def choose_kernel(token, far_top, far_bottom, out):
    del token
    own_half = lax.axis_index("col") == half(lax.axis_index("row") // 4)

    @pl.when(own_half)
    def _():
        out[...] = far_bottom[...]

    @pl.when(jnp.logical_not(own_half))
    def _():
        out[...] = far_top[...]


def choose(token, far_top, far_bottom):
    return in_vmem(choose_kernel, (like(*far_top.shape),), token, far_top, far_bottom)[0]


def after_kernel(token, *refs):
    refs[len(refs) // 2][...] = jnp.zeros((8, 128), jnp.float32)


def after(token, *arrays, cost=LIGHT):
    count = len(arrays)
    return pl.pallas_call(
        after_kernel,
        out_shape=(like(8, 128), *(like(*a.shape) for a in arrays)),
        in_specs=[VMEM] * (1 + count),
        out_specs=(VMEM,) * (1 + count),
        input_output_aliases={1 + i: 1 + i for i in range(count)},
        compiler_params=pltpu.CompilerParams(vmem_limit_bytes=2**20),
        cost_estimate=cost,
    )(token, *arrays)


def multiply_kernel(blocks, n_arrays, has_product, has_sum, *refs):
    left, arrays = refs[0], refs[1 : 1 + n_arrays]
    at = 1 + n_arrays + has_product
    if has_sum:
        mine, other = refs[at], refs[at + 1]
        at += 2
    product, token = refs[at], refs[at + 1]
    right, out, place, sems = refs[at + 2 :]
    row, core = lax.axis_index("row"), lax.axis_index("col")
    z, y, x = row // 4, (row // 2) % 2, row % 2
    ways = {
        "here": (x, y),
        "x": (1 - x, y),
        "y": (x, 1 - y),
        "first": (x ^ (1 - core), y ^ core),
        "second": (x ^ core, y ^ (1 - core)),
        "both": (1 - x, 1 - y),
    }

    def load(i, source):
        array, at, odd, way, part = source
        hi, lo = split(arrays[array][at * BLOCK : (at + 1) * BLOCK, :])
        to = pl.ds(i * BLOCK, BLOCK)
        right[to, 0:DEPTH] = hi
        right[to, DEPTH : 2 * DEPTH] = hi
        right[to, 2 * DEPTH : 3 * DEPTH] = lo
        from_x, from_y = ways[way]
        chunk = (((z + odd) % 2) * 2 + from_y) * 2 + from_x
        place[i] = (chunk * 2 + part) * BLOCK

    for i, sources in enumerate(blocks):
        if len(sources) == 2:
            own_half = core == half(z)

            @pl.when(own_half)
            def _():
                load(i, sources[0])

            @pl.when(jnp.logical_not(own_half))
            def _():
                load(i, sources[1])

        else:
            load(i, sources[0])

    if has_sum:
        token[...] = mine[...] + other[...]
    else:
        token[...] = jnp.zeros_like(token)

    def store(i, slab):
        rows = pl.ds(slab * SLAB, SLAB)
        return pltpu.make_async_copy(
            out.at[i, rows],
            product.at[rows, pl.ds(pl.multiple_of(place[i], BLOCK), BLOCK)],
            sems.at[i, slab],
        )

    slabs = left.shape[0] // SLAB

    @pl.loop(0, len(blocks))
    def _(i):
        for slab in range(slabs):
            rows = pl.ds(slab * SLAB, SLAB)
            out[i, rows] = lax.dot_general(
                left[rows, :],
                right[pl.ds(pl.multiple_of(i * BLOCK, BLOCK), BLOCK), :],
                (((1,), (1,)), ((), ())),
                preferred_element_type=jnp.float32,
            )
            store(i, slab).start()

    @pl.loop(0, len(blocks))
    def _(i):
        for slab in range(slabs):
            store(i, slab).wait()


def multiply(left, blocks, product, cols, sums=None):
    arrays, listed = [], []
    for sources in blocks:
        found = []
        for array, *rest in sources:
            known = [i for i, a in enumerate(arrays) if a is array]
            if not known:
                arrays.append(array)
            found.append((known[0] if known else len(arrays) - 1, *rest))
        listed.append(found)
    rows, count = left.shape[0], len(blocks)
    operands, in_specs = [left, *arrays], [VMEM] * (1 + len(arrays))
    aliases = {}
    if product is not None:
        aliases = {len(operands): 0}
        operands.append(product)
        in_specs.append(ANY)
    if sums is not None:
        operands += sums
        in_specs += [VMEM] * 2
    return pl.pallas_call(
        functools.partial(
            multiply_kernel, listed, len(arrays), product is not None, sums is not None
        ),
        out_shape=(
            jax.ShapeDtypeStruct((rows, cols), jnp.float32),
            jax.ShapeDtypeStruct((8, 128), jnp.float32),
        ),
        in_specs=in_specs,
        out_specs=(ANY, VMEM),
        scratch_shapes=[
            pltpu.VMEM((count * BLOCK, 3 * DEPTH), jnp.bfloat16),
            pltpu.VMEM((count, rows, BLOCK), jnp.float32),
            pltpu.SMEM((count,), jnp.int32),
            pltpu.SemaphoreType.DMA((count, rows // SLAB)),
        ],
        input_output_aliases=aliases,
        compiler_params=pltpu.CompilerParams(vmem_limit_bytes=22 * 2**20),
        cost_estimate=HEAVY,
    )(*operands)


def half(z):
    return z // 2


def moves(target):
    pairs = []
    for z in range(4):
        for y in range(2):
            for x in range(2):
                for c in range(2):
                    to = target(x, y, z, c)
                    if to is not None:
                        tx, ty, tz, tc = to
                        here = ((z * 2 + y) * 2 + x) * 2 + c
                        there = (((tz % 4) * 2 + ty) * 2 + tx) * 2 + tc
                        pairs.append((here, there))
    return pairs


CORE = moves(lambda x, y, z, c: (x, y, z, 1 - c))
FIRST = moves(lambda x, y, z, c: (1 - x, y, z, c) if c == 0 else (x, 1 - y, z, c))
SECOND = moves(lambda x, y, z, c: (x, 1 - y, z, c) if c == 0 else (1 - x, y, z, c))
Z_NEAR = moves(lambda x, y, z, c: (x, y, z + 1 if c == 1 else z - 1, half(z)))
Z_FAR = moves(
    lambda x, y, z, c: (x, y, z + 1, c) if c == half((z - 1) % 4) else None
)
Z_FAR_BY = moves(
    lambda x, y, z, c: (x, y, z + 1, 1 - c) if c == half((z - 1) % 4) else None
)
FAR_FIRST = moves(
    lambda x, y, z, c: (1 - x, y, z, c) if c != half(z) else (x, 1 - y, z, c)
)
FAR_SECOND = moves(
    lambda x, y, z, c: (x, 1 - y, z, c) if c != half(z) else (1 - x, y, z, c)
)
Z_1 = moves(lambda x, y, z, c: (x, y, z ^ 1, c))
Z_2 = moves(lambda x, y, z, c: (x, y, z ^ 2, c))


def send(name, a, pairs):
    with jax.named_scope(name):
        return lax.ppermute(a, BOTH, pairs)


def on_16x2(density):
    rows, cols = density.shape
    n = 16 * rows
    mul = functools.partial(multiply, cols=cols)

    panel = density[:, 0:PANEL]
    sib = send("sib", panel, CORE)
    raw1 = send("raw1", panel, FIRST)
    left, total, top, bottom, again = own_rows(panel, sib)
    raw2 = send("raw2", again, SECOND)
    odd_t, odd_b = send("odd_t", top, Z_NEAR), send("odd_b", bottom, Z_NEAR)

    token, raw1 = after(total, raw1)
    raw3 = send("raw3", raw1, SECOND)
    token, odd_t = after(token, odd_t)
    odd_t1, odd_t2 = send("odd_t1", odd_t, FIRST), send("odd_t2", odd_t, SECOND)
    far_t = send("far_t", odd_t, Z_FAR)
    token, raw2, raw3 = after(token, raw2, raw3)
    mine = stack(raw1, raw2, raw3)
    other = send("other", mine, CORE)
    token, odd_b = after(token, odd_b)
    odd_b1, far_b = send("odd_b1", odd_b, FIRST), send("far_b", odd_b, Z_FAR_BY)
    token, odd_t1 = after(token, odd_t1, cost=HEAVY)
    odd_t3 = send("odd_t3", odd_t1, SECOND)
    product, token = mul(
        left,
        [
            [(odd_t, 0, 1, "here", 0)],
            [(odd_t1, 0, 1, "first", 0)],
            [(odd_t2, 0, 1, "second", 0)],
        ],
        None,
        sums=(token, token),
    )
    plane, total = plane_rows(mine, other, total, token)
    far = choose(total, far_t, far_b)
    far1, far2 = send("far1", far, FAR_FIRST), send("far2", far, FAR_SECOND)
    total_1 = send("total_1", total, Z_1)
    token, odd_b1 = after(total, odd_b1)
    token, odd_b = after(token, odd_b)
    odd_b2 = send("odd_b2", odd_b, SECOND)
    token, total, total_1 = after(token, total, total_1)
    product, total = mul(
        left,
        [
            [(odd_t3, 0, 1, "both", 0)],
            [(odd_b, 0, 1, "here", 1)],
            [(odd_b1, 0, 1, "first", 1)],
        ],
        product,
        sums=(total, total_1),
    )
    total_2 = send("total_2", total, Z_2)
    token, total_2 = after(total, total_2)
    token, far1 = after(token, far1)
    far3 = send("far3", far1, FAR_SECOND)
    token, odd_b1 = after(token, odd_b1)
    odd_b3 = send("odd_b3", odd_b1, SECOND)
    token, odd_b2 = after(token, odd_b2)
    token, far2 = after(token, far2)
    far_mine = stack(far, far1, far2)
    far_other = send("far_other", far_mine, CORE)
    product, total = mul(
        left,
        [
            [(top, 0, 0, "here", 0), (far_mine, 0, 0, "here", 0)],
            [(bottom, 0, 0, "here", 1), (far_other, 0, 0, "here", 1)],
            [(plane, 0, 0, "first", 0), (far_mine, 1, 0, "x", 0)],
            [(plane, 1, 0, "first", 1), (far_other, 1, 0, "y", 1)],
            [(plane, 2, 0, "second", 0), (far_mine, 2, 0, "y", 0)],
            [(plane, 3, 0, "second", 1), (far_other, 2, 0, "x", 1)],
        ],
        product,
        sums=(total, total_2),
    )
    occupation = total[0, 0] / (n * math.sqrt(DEPTH))
    token, odd_b3 = after(total, odd_b3)
    token, far3 = after(token, far3)
    far3_other = send("far3_other", far3, CORE)
    product, token = mul(
        left,
        [
            [(odd_b2, 0, 1, "second", 1)],
            [(odd_b3, 0, 1, "both", 1)],
            [(plane, 4, 0, "both", 0), (far3, 0, 0, "both", 0)],
            [(plane, 5, 0, "both", 1), (far3_other, 0, 0, "both", 1)],
        ],
        product,
    )
    return product, jnp.reshape(occupation, (1,))


def on_any(n, density):
    rows, cols = density.shape
    core = lax.axis_index("col")
    pieces = []
    for step in range(STEPS):
        start = step * (n // STEPS)
        at = start % cols
        piece = density[:, at : at + PANEL]
        pieces.append(jnp.where(core == start // cols, piece, 0.0))
    panel = lax.psum(jnp.concatenate(pieces, axis=1), "col")
    occupation = lax.psum(jnp.sum(panel * panel), "row") / (n * math.sqrt(DEPTH))
    whole = lax.all_gather(panel, "row", tiled=True)
    mine = lax.dynamic_slice_in_dim(whole, core * cols, cols, axis=0)
    product = lax.dot_general(
        panel,
        mine,
        (((1,), (1,)), ((), ())),
        precision=lax.Precision.HIGHEST,
        preferred_element_type=jnp.float32,
    )
    return product, jnp.reshape(occupation, (1,))


def solution(mesh):
    sizes = (mesh.shape["row"], mesh.shape["col"])

    def run(density):
        n = density.shape[0]
        body = functools.partial(on_any, n)
        if sizes == (16, 2) and n == 16 * 2 * BLOCK:
            body = on_16x2
        return jax.shard_map(
            body,
            mesh=mesh,
            in_specs=(P("row", "col"),),
            out_specs=(P("row", "col"), P()),
            check_vma=False,
        )(density)

    return run
```

time: 103 us -> 91.6 us (0.89)
  the two profiles are of different devices: /device:TPU:16 before, /device:TPU:1 now
where the time goes in v2:
time: 91.6 us; the launch traced here: 90.9 us
  starting transfers between devices  30.4 us (33%)
  waiting for transfers between devices  30.3 us (33%)
  Pallas kernels  26.1 us (28%)
  between operations  2.54 us (3%)
  local copies, waits for them, and re-layouts  1.59 us (2%)
    ppermute x22, starting transfers between devices, send(): return lax.ppermute(a, BOTH, pairs)  30.4 us
    ppermute x22, waiting for transfers between devices, send(): return lax.ppermute(a, BOTH, pairs)  30.3 us
    pallas_call x4, Pallas kernels, multiply(): pl.pallas_call(functools.partial(multiply_kernel, listed, len(arrays), pr...  22.5 us
    pallas_call x5, Pallas kernels, in_vmem(): pl.pallas_call(kernel, out_shape=out_shape, in_specs=[VMEM] * len(arrays)...  1.86 us
  transfers between devices with their start and end apart: 22, of which 10 were waited for; matrix products, arithmetic and copies ran while one was open for 1% of the time, Pallas kernels for 21%

profile of v2, /device:TPU:1, one launch (start us, length us, event | category | flops | bytes accessed | tf_op | source)
XLA Modules:
  0.0 90.9 jit_solution(6677147085948779512)
XLA Ops:
  0.6 1.1 %slice.6.mine = f32[1024,128]{1,0:T(8,128)S(1)} slice(f32[1024,8192]{1,0:T(8,128)} %param.1), slice={[0:1024], [0:128]} | slice | bytes 1048576 | tf_op jit(solution)/shard_map/slice | solution.py:300
  1.7 0.1 collective-permute-start
  1.8 2.7 %collective-permute-start.1 = (f32[1024,128]{1,0:T(8,128)S(1)}, f32[1024,128]{1,0:T(8,128)S(1)}, u32[]{:S(2)}, u32[]{:S(2)}) collective-permute-start(f32[1024,128]{1,0:T(8,128)S(1)} %slice.6.mine), channel_id=1, source_target_pairs={{0,2},{1,5},{2,0},{3,7},{4,6},{5,1},{6,4},{7,3},{8,10},{9,13},{10,... | collective-permute-start | bytes 1572872 | tf_op jit(solution)/shard_map/raw1/ppermute | solution.py:292
  4.5 0.9 shard_map.30
  5.4 1.9 %collective-permute-start.2 = (f32[512,256]{1,0:T(8,128)S(1)}, f32[512,256]{1,0:T(8,128)S(1)}, u32[]{:S(2)}, u32[]{:S(2)}) collective-permute-start(f32[512,256]{1,0:T(8,128)S(1)} %get-tuple-element.48.refs_1_), channel_id=1, source_target_pairs={{0,24},{1,8},{2,26},{3,10},{4,28},{5,12},{6,30},{7,14},{8,0},{9,16... | collective-permute-start | bytes 1572872 | tf_op jit(solution)/shard_map/odd_t/ppermute | solution.py:292
  7.3 4.1 %collective-permute-done.1.refs_0_ = f32[1024,128]{1,0:T(8,128)S(1)} collective-permute-done((f32[1024,128]{1,0:T(8,128)S(1)}, f32[1024,128]{1,0:T(8,128)S(1)}, u32[]{:S(2)}, u32[]{:S(2)}) %collective-permute-start.1) | collective-permute-done | bytes 524320 | tf_op jit(solution)/shard_map/raw1/ppermute | solution.py:292
  11.4 1.4 %collective-permute-start.4 = (f32[1024,128]{1,0:T(8,128)S(1)}, f32[1024,128]{1,0:T(8,128)S(1)}, u32[]{:S(2)}, u32[]{:S(2)}) collective-permute-start(f32[1024,128]{1,0:T(8,128)S(1)} %get-tuple-element.51.refs_0_), channel_id=1, source_target_pairs={{0,4},{1,3},{2,6},{3,1},{4,0},{5,7},{6,2},{7,5},{8,12},{9,11},{10,... | collective-permute-start | bytes 1572872 | tf_op jit(solution)/shard_map/raw3/ppermute | solution.py:292
  12.8 0.0 collective-permute-start.3
  12.9 2.9 %collective-permute-start.5 = (f32[512,256]{1,0:T(8,128)S(1)}, f32[512,256]{1,0:T(8,128)S(1)}, u32[]{:S(2)}, u32[]{:S(2)}) collective-permute-start(f32[512,256]{1,0:T(8,128)S(1)} %get-tuple-element.53.refs_3_), channel_id=1, source_target_pairs={{0,24},{1,8},{2,26},{3,10},{4,28},{5,12},{6,30},{7,14},{8,0},{9,16... | collective-permute-start | bytes 1572872 | tf_op jit(solution)/shard_map/odd_b/ppermute | solution.py:292
  15.8 4.8 %collective-permute-done.2.refs_0_ = f32[512,256]{1,0:T(8,128)S(1)} collective-permute-done((f32[512,256]{1,0:T(8,128)S(1)}, f32[512,256]{1,0:T(8,128)S(1)}, u32[]{:S(2)}, u32[]{:S(2)}) %collective-permute-start.2) | collective-permute-done | bytes 524320 | tf_op jit(solution)/shard_map/odd_t/ppermute | solution.py:292
  20.6 1.2 %collective-permute-start.6 = (f32[512,256]{1,0:T(8,128)S(1)}, f32[512,256]{1,0:T(8,128)S(1)}, u32[]{:S(2)}, u32[]{:S(2)}) collective-permute-start(f32[512,256]{1,0:T(8,128)S(1)} %get-tuple-element.55.refs_1_), channel_id=1, source_target_pairs={{0,2},{1,5},{2,0},{3,7},{4,6},{5,1},{6,4},{7,3},{8,10},{9,13},{10,... | collective-permute-start | bytes 1572872 | tf_op jit(solution)/shard_map/odd_t1/ppermute | solution.py:292
  21.8 3.3 %collective-permute-start.13 = (f32[512,256]{1,0:T(8,128)S(1)}, f32[512,256]{1,0:T(8,128)S(1)}, u32[]{:S(2)}, u32[]{:S(2)}) collective-permute-start(f32[512,256]{1,0:T(8,128)S(1)} %get-tuple-element.55.refs_1_), channel_id=1, source_target_pairs={{1,9},{3,11},{5,13},{7,15},{8,16},{10,18},{12,20},{14,22},{16,24},... | collective-permute-start | bytes 1572872 | tf_op jit(solution)/shard_map/far_t/ppermute | solution.py:292
  25.1 0.0 collective-permute-done.4.refs_1_
  25.1 1.3 %collective-permute-start.9 = (f32[512,256]{1,0:T(8,128)S(1)}, f32[512,256]{1,0:T(8,128)S(1)}, u32[]{:S(2)}, u32[]{:S(2)}) collective-permute-start(f32[512,256]{1,0:T(8,128)S(1)} %get-tuple-element.55.refs_1_), channel_id=1, source_target_pairs={{0,4},{1,3},{2,6},{3,1},{4,0},{5,7},{6,2},{7,5},{8,12},{9,11},{10,... | collective-permute-start | bytes 1572872 | tf_op jit(solution)/shard_map/odd_t2/ppermute | solution.py:292
  26.4 0.0 collective-permute-done.3.refs_0_
  26.4 5.4 %collective-permute-done.5.refs_0_ = f32[512,256]{1,0:T(8,128)S(1)} collective-permute-done((f32[512,256]{1,0:T(8,128)S(1)}, f32[512,256]{1,0:T(8,128)S(1)}, u32[]{:S(2)}, u32[]{:S(2)}) %collective-permute-start.5) | collective-permute-done | bytes 524320 | tf_op jit(solution)/shard_map/odd_b/ppermute | solution.py:292
  31.8 2.2 %collective-permute-start.14 = (f32[512,256]{1,0:T(8,128)S(1)}, f32[512,256]{1,0:T(8,128)S(1)}, u32[]{:S(2)}, u32[]{:S(2)}) collective-permute-start(f32[512,256]{1,0:T(8,128)S(1)} %get-tuple-element.62.refs_0_), channel_id=1, source_target_pairs={{1,8},{3,10},{5,12},{7,14},{8,17},{10,19},{12,21},{14,23},{16,25},... | collective-permute-start | bytes 1572872 | tf_op jit(solution)/shard_map/far_b/ppermute | solution.py:292
  34.0 1.3 %collective-permute-start.10 = (f32[512,256]{1,0:T(8,128)S(1)}, f32[512,256]{1,0:T(8,128)S(1)}, u32[]{:S(2)}, u32[]{:S(2)}) collective-permute-start(f32[512,256]{1,0:T(8,128)S(1)} %get-tuple-element.62.refs_0_), channel_id=1, source_target_pairs={{0,2},{1,5},{2,0},{3,7},{4,6},{5,1},{6,4},{7,3},{8,10},{9,13},{10,... | collective-permute-start | bytes 1572872 | tf_op jit(solution)/shard_map/odd_b1/ppermute | solution.py:292
  35.3 0.1 shard_map.36.mine
  35.4 1.0 %collective-permute-start.8 = (f32[3072,128]{1,0:T(8,128)S(1)}, f32[3072,128]{1,0:T(8,128)S(1)}, u32[]{:S(2)}, u32[]{:S(2)}) collective-permute-start(f32[3072,128]{1,0:T(8,128)S(1)} %shard_map.36.mine), channel_id=1, source_target_pairs={{0,1},{1,0},{2,3},{3,2},{4,5},{5,4},{6,7},{7,6},{8,9},{9,8},{10,11... | collective-permute-start | bytes 4718600 | tf_op jit(solution)/shard_map/other/ppermute | solution.py:292
  36.4 0.2 collective-permute-done.9.refs_3_
  36.6 1.4 %collective-permute-start.7 = (f32[512,256]{1,0:T(8,128)S(1)}, f32[512,256]{1,0:T(8,128)S(1)}, u32[]{:S(2)}, u32[]{:S(2)}) collective-permute-start(f32[512,256]{1,0:T(8,128)S(1)} %get-tuple-element.56.refs_2_), channel_id=1, source_target_pairs={{0,4},{1,3},{2,6},{3,1},{4,0},{5,7},{6,2},{7,5},{8,12},{9,11},{10,... | collective-permute-start | bytes 1572872 | tf_op jit(solution)/shard_map/odd_t3/ppermute | solution.py:292
  38.0 4.4 %shard_map.37 = (f32[1024,8192]{1,0:T(8,128)}, f32[8,128]{1,0:T(8,128)S(1)}) custom-call(bf16[1024,768]{1,0:T(8,128)(2,1)S(1)} %get-tuple-element.45.refs_0_, f32[512,256]{1,0:T(8,128)S(1)} %get-tuple-element.55.refs_1_, f32[512,256]{1,0:T(8,128)S(1)} %get-tuple-element.56.refs_2_, f32[512,256]{1,0:T(8,128)S(1)} %collective-permute-done.9.refs_3_, ...), custom_call_target="tpu_custom_call" | custom-call | flops 10000000000 | bytes 100000000 | tf_op jit(solution)/shard_map/pallas_call | solution.py:229
  42.4 0.0 collective-permute-done.8.other
  42.4 0.8 shard_map.38
  43.1 1.4 %collective-permute-start.11 = (f32[8,128]{1,0:T(8,128)S(1)}, f32[8,128]{1,0:T(8,128)S(1)}, u32[]{:S(2)}, u32[]{:S(2)}) collective-permute-start(f32[8,128]{1,0:T(8,128)S(1)} %get-tuple-element.61.token.refs_0_), channel_id=1, source_target_pairs={{0,8},{1,9},{2,10},{3,11},{4,12},{5,13},{6,14},{7,15},{8,0},{9,1},... | collective-permute-start | bytes 12296 | tf_op jit(solution)/shard_map/total_1/ppermute | solution.py:292
  44.6 1.3 %collective-permute-start.17 = (f32[512,256]{1,0:T(8,128)S(1)}, f32[512,256]{1,0:T(8,128)S(1)}, u32[]{:S(2)}, u32[]{:S(2)}) collective-permute-start(f32[512,256]{1,0:T(8,128)S(1)} %shard_map.44.refs_0_), channel_id=1, source_target_pairs={{0,2},{1,5},{2,0},{3,7},{4,6},{5,1},{6,4},{7,3},{8,10},{9,13},{10,... | collective-permute-start | bytes 1572872 | tf_op jit(solution)/shard_map/far2/ppermute | solution.py:292
  45.9 0.3 collective-permute-start.15
  46.1 1.2 %collective-permute-start.16 = (f32[512,256]{1,0:T(8,128)S(1)}, f32[512,256]{1,0:T(8,128)S(1)}, u32[]{:S(2)}, u32[]{:S(2)}) collective-permute-start(f32[512,256]{1,0:T(8,128)S(1)} %get-tuple-element.64.refs_2_), channel_id=1, source_target_pairs={{0,4},{1,3},{2,6},{3,1},{4,0},{5,7},{6,2},{7,5},{8,12},{9,11},{10,... | collective-permute-start | bytes 1572872 | tf_op jit(solution)/shard_map/odd_b2/ppermute | solution.py:292
  47.3 0.6 shard_map.41
  47.9 1.2 %collective-permute-done.7.refs_1_ = f32[512,256]{1,0:T(8,128)S(1)} collective-permute-done((f32[512,256]{1,0:T(8,128)S(1)}, f32[512,256]{1,0:T(8,128)S(1)}, u32[]{:S(2)}, u32[]{:S(2)}) %collective-permute-start.7) | collective-permute-done | bytes 524320 | tf_op jit(solution)/shard_map/odd_t3/ppermute | solution.py:292
  49.1 4.4 %shard_map.42 = (f32[1024,8192]{1,0:T(8,128)}, f32[8,128]{1,0:T(8,128)S(1)}) custom-call(bf16[1024,768]{1,0:T(8,128)(2,1)S(1)} %get-tuple-element.45.refs_0_, f32[512,256]{1,0:T(8,128)S(1)} %collective-permute-done.7.refs_1_, f32[512,256]{1,0:T(8,128)S(1)} %get-tuple-element.64.refs_2_, ...), custom_call_target="tpu_custom_call", output_to_operand_aliasing={{0}: (4, {})} | custom-call | flops 10000000000 | bytes 100000000 | tf_op jit(solution)/shard_map/pallas_call | solution.py:229
  53.4 1.6 %collective-permute-start.12 = (f32[8,128]{1,0:T(8,128)S(1)}, f32[8,128]{1,0:T(8,128)S(1)}, u32[]{:S(2)}, u32[]{:S(2)}) collective-permute-start(f32[8,128]{1,0:T(8,128)S(1)} %get-tuple-element.70.token.refs_7_), channel_id=1, source_target_pairs={{0,16},{1,17},{2,18},{3,19},{4,20},{5,21},{6,22},{7,23},{8,24},{9,... | collective-permute-start | bytes 12296 | tf_op jit(solution)/shard_map/total_2/ppermute | solution.py:292
  55.1 1.8 %collective-permute-done.12.refs_0_ = f32[8,128]{1,0:T(8,128)S(1)} collective-permute-done((f32[8,128]{1,0:T(8,128)S(1)}, f32[8,128]{1,0:T(8,128)S(1)}, u32[]{:S(2)}, u32[]{:S(2)}) %collective-permute-start.12) | collective-permute-done | bytes 4128 | tf_op jit(solution)/shard_map/total_2/ppermute | solution.py:292
  56.9 8.9 %collective-permute-done.16.refs_0_ = f32[512,256]{1,0:T(8,128)S(1)} collective-permute-done((f32[512,256]{1,0:T(8,128)S(1)}, f32[512,256]{1,0:T(8,128)S(1)}, u32[]{:S(2)}, u32[]{:S(2)}) %collective-permute-start.16) | collective-permute-done | bytes 524320 | tf_op jit(solution)/shard_map/odd_b2/ppermute | solution.py:292
  65.8 0.6 shard_map.48
  66.4 0.1 shard_map.49.refs_2_
  66.5 0.5 collective-permute-start.18
  66.9 1.7 %collective-permute-start.20 = (f32[512,256]{1,0:T(8,128)S(1)}, f32[512,256]{1,0:T(8,128)S(1)}, u32[]{:S(2)}, u32[]{:S(2)}) collective-permute-start(f32[512,256]{1,0:T(8,128)S(1)} %get-tuple-element.75.refs_1_), channel_id=1, source_target_pairs={{0,2},{1,5},{2,0},{3,7},{4,6},{5,1},{6,4},{7,3},{8,10},{9,13},{10,... | collective-permute-start | bytes 1572872 | tf_op jit(solution)/shard_map/far3/ppermute | solution.py:292
  68.7 1.2 %collective-permute-start.19 = (f32[512,256]{1,0:T(8,128)S(1)}, f32[512,256]{1,0:T(8,128)S(1)}, u32[]{:S(2)}, u32[]{:S(2)}) collective-permute-start(f32[512,256]{1,0:T(8,128)S(1)} %get-tuple-element.82), channel_id=1, source_target_pairs={{0,4},{1,3},{2,6},{3,1},{4,0},{5,7},{6,2},{7,5},{8,12},{9,11},{10,... | collective-permute-start | bytes 1572872 | tf_op jit(solution)/shard_map/odd_b3/ppermute | solution.py:292
  69.9 0.1 collective-permute-done.18.refs_4_
  70.0 7.7 %shard_map.50 = (f32[1024,8192]{1,0:T(8,128)}, f32[8,128]{1,0:T(8,128)S(1)}) custom-call(bf16[1024,768]{1,0:T(8,128)(2,1)S(1)} %get-tuple-element.45.refs_0_, f32[512,256]{1,0:T(8,128)S(1)} %get-tuple-element.48.refs_1_, f32[1536,256]{1,0:T(8,128)S(1)} %shard_map.49.refs_2_, ...), custom_call_target="tpu_custom_call", output_to_operand_aliasing={{0}: (6, {})} | custom-call | flops 10000000000 | bytes 100000000 | tf_op jit(solution)/shard_map/pallas_call | solution.py:229
  77.7 3.5 %collective-permute-done.19.refs_0_ = f32[512,256]{1,0:T(8,128)S(1)} collective-permute-done((f32[512,256]{1,0:T(8,128)S(1)}, f32[512,256]{1,0:T(8,128)S(1)}, u32[]{:S(2)}, u32[]{:S(2)}) %collective-permute-start.19) | collective-permute-done | bytes 524320 | tf_op jit(solution)/shard_map/odd_b3/ppermute | solution.py:292
  81.2 0.6 shard_map.52
  81.8 0.4 collective-permute-start.21
  82.2 0.5 slice.7
  83.3 0.4 collective-permute-done.21.refs_5_
  83.7 6.1 %shard_map.53 = (f32[1024,8192]{1,0:T(8,128)}, f32[8,128]{1,0:T(8,128)}) custom-call(bf16[1024,768]{1,0:T(8,128)(2,1)S(1)} %get-tuple-element.45.refs_0_, f32[512,256]{1,0:T(8,128)S(1)} %get-tuple-element.74.refs_1_, f32[512,256]{1,0:T(8,128)S(1)} %get-tuple-element.83.refs_2_, ...), custom_call_target="tpu_custom_call", output_to_operand_aliasing={{0}: (6, {})} | custom-call | flops 10000000000 | bytes 100000000 | tf_op jit(solution)/shard_map/pallas_call | solution.py:229
  (22 shorter events, 0.1 us)
Async XLA Ops:
  1.7 2.8 %collective-permute-start = (f32[1024,128]{1,0:T(8,128)S(1)}, f32[1024,128]{1,0:T(8,128)S(1)}, u32[]{:S(2)}, u32[]{:S(2)}) collective-permute-start(f32[1024,128]{1,0:T(8,128)S(1)} %slice.6.mine), channel_id=1, source_target_pairs={{0,1},{1,0},{2,3},{3,2},{4,5},{5,4},{6,7},{7,6},{8,9},{9,8},{10,11... | collective-permute-start | bytes 1572872 | tf_op jit(solution)/shard_map/sib/ppermute | solution.py:292
  1.8 9.6 %collective-permute-start.1 = (f32[1024,128]{1,0:T(8,128)S(1)}, f32[1024,128]{1,0:T(8,128)S(1)}, u32[]{:S(2)}, u32[]{:S(2)}) collective-permute-start(f32[1024,128]{1,0:T(8,128)S(1)} %slice.6.mine), channel_id=1, source_target_pairs={{0,2},{1,5},{2,0},{3,7},{4,6},{5,1},{6,4},{7,3},{8,10},{9,13},{10,... | collective-permute-start | bytes 1572872 | tf_op jit(solution)/shard_map/raw1/ppermute | solution.py:292
  5.4 15.2 %collective-permute-start.2 = (f32[512,256]{1,0:T(8,128)S(1)}, f32[512,256]{1,0:T(8,128)S(1)}, u32[]{:S(2)}, u32[]{:S(2)}) collective-permute-start(f32[512,256]{1,0:T(8,128)S(1)} %get-tuple-element.48.refs_1_), channel_id=1, source_target_pairs={{0,24},{1,8},{2,26},{3,10},{4,28},{5,12},{6,30},{7,14},{8,0},{9,16... | collective-permute-start | bytes 1572872 | tf_op jit(solution)/shard_map/odd_t/ppermute | solution.py:292
  11.4 13.7 %collective-permute-start.4 = (f32[1024,128]{1,0:T(8,128)S(1)}, f32[1024,128]{1,0:T(8,128)S(1)}, u32[]{:S(2)}, u32[]{:S(2)}) collective-permute-start(f32[1024,128]{1,0:T(8,128)S(1)} %get-tuple-element.51.refs_0_), channel_id=1, source_target_pairs={{0,4},{1,3},{2,6},{3,1},{4,0},{5,7},{6,2},{7,5},{8,12},{9,11},{10,... | collective-permute-start | bytes 1572872 | tf_op jit(solution)/shard_map/raw3/ppermute | solution.py:292
  12.8 13.6 %collective-permute-start.3 = (f32[1024,128]{1,0:T(8,128)S(1)}, f32[1024,128]{1,0:T(8,128)S(1)}, u32[]{:S(2)}, u32[]{:S(2)}) collective-permute-start(f32[1024,128]{1,0:T(8,128)S(1)} %get-tuple-element.50), channel_id=1, source_target_pairs={{0,4},{1,3},{2,6},{3,1},{4,0},{5,7},{6,2},{7,5},{8,12},{9,11},{10,... | collective-permute-start | bytes 1572872 | tf_op jit(solution)/shard_map/raw2/ppermute | solution.py:292
  12.9 18.9 %collective-permute-start.5 = (f32[512,256]{1,0:T(8,128)S(1)}, f32[512,256]{1,0:T(8,128)S(1)}, u32[]{:S(2)}, u32[]{:S(2)}) collective-permute-start(f32[512,256]{1,0:T(8,128)S(1)} %get-tuple-element.53.refs_3_), channel_id=1, source_target_pairs={{0,24},{1,8},{2,26},{3,10},{4,28},{5,12},{6,30},{7,14},{8,0},{9,16... | collective-permute-start | bytes 1572872 | tf_op jit(solution)/shard_map/odd_b/ppermute | solution.py:292
  20.6 14.8 %collective-permute-start.6 = (f32[512,256]{1,0:T(8,128)S(1)}, f32[512,256]{1,0:T(8,128)S(1)}, u32[]{:S(2)}, u32[]{:S(2)}) collective-permute-start(f32[512,256]{1,0:T(8,128)S(1)} %get-tuple-element.55.refs_1_), channel_id=1, source_target_pairs={{0,2},{1,5},{2,0},{3,7},{4,6},{5,1},{6,4},{7,3},{8,10},{9,13},{10,... | collective-permute-start | bytes 1572872 | tf_op jit(solution)/shard_map/odd_t1/ppermute | solution.py:292
  21.8 22.7 %collective-permute-start.13 = (f32[512,256]{1,0:T(8,128)S(1)}, f32[512,256]{1,0:T(8,128)S(1)}, u32[]{:S(2)}, u32[]{:S(2)}) collective-permute-start(f32[512,256]{1,0:T(8,128)S(1)} %get-tuple-element.55.refs_1_), channel_id=1, source_target_pairs={{1,9},{3,11},{5,13},{7,15},{8,16},{10,18},{12,20},{14,22},{16,24},... | collective-permute-start | bytes 1572872 | tf_op jit(solution)/shard_map/far_t/ppermute | solution.py:292
  25.1 11.4 %collective-permute-start.9 = (f32[512,256]{1,0:T(8,128)S(1)}, f32[512,256]{1,0:T(8,128)S(1)}, u32[]{:S(2)}, u32[]{:S(2)}) collective-permute-start(f32[512,256]{1,0:T(8,128)S(1)} %get-tuple-element.55.refs_1_), channel_id=1, source_target_pairs={{0,4},{1,3},{2,6},{3,1},{4,0},{5,7},{6,2},{7,5},{8,12},{9,11},{10,... | collective-permute-start | bytes 1572872 | tf_op jit(solution)/shard_map/odd_t2/ppermute | solution.py:292
  31.8 12.7 %collective-permute-start.14 = (f32[512,256]{1,0:T(8,128)S(1)}, f32[512,256]{1,0:T(8,128)S(1)}, u32[]{:S(2)}, u32[]{:S(2)}) collective-permute-start(f32[512,256]{1,0:T(8,128)S(1)} %get-tuple-element.62.refs_0_), channel_id=1, source_target_pairs={{1,8},{3,10},{5,12},{7,14},{8,17},{10,19},{12,21},{14,23},{16,25},... | collective-permute-start | bytes 1572872 | tf_op jit(solution)/shard_map/far_b/ppermute | solution.py:292
  34.0 12.2 %collective-permute-start.10 = (f32[512,256]{1,0:T(8,128)S(1)}, f32[512,256]{1,0:T(8,128)S(1)}, u32[]{:S(2)}, u32[]{:S(2)}) collective-permute-start(f32[512,256]{1,0:T(8,128)S(1)} %get-tuple-element.62.refs_0_), channel_id=1, source_target_pairs={{0,2},{1,5},{2,0},{3,7},{4,6},{5,1},{6,4},{7,3},{8,10},{9,13},{10,... | collective-permute-start | bytes 1572872 | tf_op jit(solution)/shard_map/odd_b1/ppermute | solution.py:292
  35.4 7.0 %collective-permute-start.8 = (f32[3072,128]{1,0:T(8,128)S(1)}, f32[3072,128]{1,0:T(8,128)S(1)}, u32[]{:S(2)}, u32[]{:S(2)}) collective-permute-start(f32[3072,128]{1,0:T(8,128)S(1)} %shard_map.36.mine), channel_id=1, source_target_pairs={{0,1},{1,0},{2,3},{3,2},{4,5},{5,4},{6,7},{7,6},{8,9},{9,8},{10,11... | collective-permute-start | bytes 4718600 | tf_op jit(solution)/shard_map/other/ppermute | solution.py:292
  36.6 12.5 %collective-permute-start.7 = (f32[512,256]{1,0:T(8,128)S(1)}, f32[512,256]{1,0:T(8,128)S(1)}, u32[]{:S(2)}, u32[]{:S(2)}) collective-permute-start(f32[512,256]{1,0:T(8,128)S(1)} %get-tuple-element.56.refs_2_), channel_id=1, source_target_pairs={{0,4},{1,3},{2,6},{3,1},{4,0},{5,7},{6,2},{7,5},{8,12},{9,11},{10,... | collective-permute-start | bytes 1572872 | tf_op jit(solution)/shard_map/odd_t3/ppermute | solution.py:292
  43.1 4.2 %collective-permute-start.11 = (f32[8,128]{1,0:T(8,128)S(1)}, f32[8,128]{1,0:T(8,128)S(1)}, u32[]{:S(2)}, u32[]{:S(2)}) collective-permute-start(f32[8,128]{1,0:T(8,128)S(1)} %get-tuple-element.61.token.refs_0_), channel_id=1, source_target_pairs={{0,8},{1,9},{2,10},{3,11},{4,12},{5,13},{6,14},{7,15},{8,0},{9,1},... | collective-permute-start | bytes 12296 | tf_op jit(solution)/shard_map/total_1/ppermute | solution.py:292
  44.6 21.2 %collective-permute-start.17 = (f32[512,256]{1,0:T(8,128)S(1)}, f32[512,256]{1,0:T(8,128)S(1)}, u32[]{:S(2)}, u32[]{:S(2)}) collective-permute-start(f32[512,256]{1,0:T(8,128)S(1)} %shard_map.44.refs_0_), channel_id=1, source_target_pairs={{0,2},{1,5},{2,0},{3,7},{4,6},{5,1},{6,4},{7,3},{8,10},{9,13},{10,... | collective-permute-start | bytes 1572872 | tf_op jit(solution)/shard_map/far2/ppermute | solution.py:292
  45.9 11.0 %collective-permute-start.15 = (f32[512,256]{1,0:T(8,128)S(1)}, f32[512,256]{1,0:T(8,128)S(1)}, u32[]{:S(2)}, u32[]{:S(2)}) collective-permute-start(f32[512,256]{1,0:T(8,128)S(1)} %shard_map.44.refs_0_), channel_id=1, source_target_pairs={{0,4},{1,3},{2,6},{3,1},{4,0},{5,7},{6,2},{7,5},{8,12},{9,11},{10,... | collective-permute-start | bytes 1572872 | tf_op jit(solution)/shard_map/far1/ppermute | solution.py:292
  46.1 19.6 %collective-permute-start.16 = (f32[512,256]{1,0:T(8,128)S(1)}, f32[512,256]{1,0:T(8,128)S(1)}, u32[]{:S(2)}, u32[]{:S(2)}) collective-permute-start(f32[512,256]{1,0:T(8,128)S(1)} %get-tuple-element.64.refs_2_), channel_id=1, source_target_pairs={{0,4},{1,3},{2,6},{3,1},{4,0},{5,7},{6,2},{7,5},{8,12},{9,11},{10,... | collective-permute-start | bytes 1572872 | tf_op jit(solution)/shard_map/odd_b2/ppermute | solution.py:292
  53.4 3.4 %collective-permute-start.12 = (f32[8,128]{1,0:T(8,128)S(1)}, f32[8,128]{1,0:T(8,128)S(1)}, u32[]{:S(2)}, u32[]{:S(2)}) collective-permute-start(f32[8,128]{1,0:T(8,128)S(1)} %get-tuple-element.70.token.refs_7_), channel_id=1, source_target_pairs={{0,16},{1,17},{2,18},{3,19},{4,20},{5,21},{6,22},{7,23},{8,24},{9,... | collective-permute-start | bytes 12296 | tf_op jit(solution)/shard_map/total_2/ppermute | solution.py:292
  66.5 3.5 %collective-permute-start.18 = (f32[1536,256]{1,0:T(8,128)S(1)}, f32[1536,256]{1,0:T(8,128)S(1)}, u32[]{:S(2)}, u32[]{:S(2)}) collective-permute-start(f32[1536,256]{1,0:T(8,128)S(1)} %shard_map.49.refs_2_), channel_id=1, source_target_pairs={{0,1},{1,0},{2,3},{3,2},{4,5},{5,4},{6,7},{7,6},{8,9},{9,8},{10,11... | collective-permute-start | bytes 4718600 | tf_op jit(solution)/shard_map/far_other/ppermute | solution.py:292
  66.9 14.2 %collective-permute-start.20 = (f32[512,256]{1,0:T(8,128)S(1)}, f32[512,256]{1,0:T(8,128)S(1)}, u32[]{:S(2)}, u32[]{:S(2)}) collective-permute-start(f32[512,256]{1,0:T(8,128)S(1)} %get-tuple-element.75.refs_1_), channel_id=1, source_target_pairs={{0,2},{1,5},{2,0},{3,7},{4,6},{5,1},{6,4},{7,3},{8,10},{9,13},{10,... | collective-permute-start | bytes 1572872 | tf_op jit(solution)/shard_map/far3/ppermute | solution.py:292
  68.7 12.5 %collective-permute-start.19 = (f32[512,256]{1,0:T(8,128)S(1)}, f32[512,256]{1,0:T(8,128)S(1)}, u32[]{:S(2)}, u32[]{:S(2)}) collective-permute-start(f32[512,256]{1,0:T(8,128)S(1)} %get-tuple-element.82), channel_id=1, source_target_pairs={{0,4},{1,3},{2,6},{3,1},{4,0},{5,7},{6,2},{7,5},{8,12},{9,11},{10,... | collective-permute-start | bytes 1572872 | tf_op jit(solution)/shard_map/odd_b3/ppermute | solution.py:292
  81.8 1.9 %collective-permute-start.21 = (f32[512,256]{1,0:T(8,128)S(1)}, f32[512,256]{1,0:T(8,128)S(1)}, u32[]{:S(2)}, u32[]{:S(2)}) collective-permute-start(f32[512,256]{1,0:T(8,128)S(1)} %get-tuple-element.85.refs_4_), channel_id=1, source_target_pairs={{0,1},{1,0},{2,3},{3,2},{4,5},{5,4},{6,7},{7,6},{8,9},{9,8},{10,11... | collective-permute-start | bytes 1572872 | tf_op jit(solution)/shard_map/far3_other/ppermute | solution.py:292

commit v3 on v2

--- a/solution.py
+++ b/solution.py
@@ -112,7 +112,11 @@
 
 
 def after_kernel(token, *refs):
-    refs[len(refs) // 2][...] = jnp.zeros((8, 128), jnp.float32)
+    del token
+    count = len(refs) // 2
+    refs[count][...] = jnp.zeros((8, 128), jnp.float32)
+    for before, later in zip(refs[:count], refs[count + 1 :], strict=True):
+        later[...] = before[...]
 
 
 def after(token, *arrays, cost=LIGHT):
@@ -123,9 +127,23 @@
         in_specs=[VMEM] * (1 + count),
         out_specs=(VMEM,) * (1 + count),
         input_output_aliases={1 + i: 1 + i for i in range(count)},
-        compiler_params=pltpu.CompilerParams(vmem_limit_bytes=2**20),
+        compiler_params=pltpu.CompilerParams(vmem_limit_bytes=2 * 2**20),
         cost_estimate=cost,
     )(token, *arrays)
+
+
+def scaled(total, factor):
+    def kernel(total_ref, out_ref):
+        out_ref[0] = jnp.max(total_ref[0:1, 0:1]) * factor
+
+    return pl.pallas_call(
+        kernel,
+        out_shape=jax.ShapeDtypeStruct((1,), jnp.float32),
+        in_specs=[VMEM],
+        out_specs=pl.BlockSpec(memory_space=pltpu.SMEM),
+        compiler_params=pltpu.CompilerParams(vmem_limit_bytes=2**20),
+        cost_estimate=LIGHT,
+    )(total)
 
 
 def multiply_kernel(blocks, n_arrays, has_product, has_sum, *refs):
@@ -206,7 +224,7 @@
             store(i, slab).wait()
 
 
-def multiply(left, blocks, product, cols, sums=None):
+def multiply(left, blocks, product, cols, sums=None, cost=HEAVY):
     arrays, listed = [], []
     for sources in blocks:
         found = []
@@ -243,8 +261,8 @@
             pltpu.SemaphoreType.DMA((count, rows // SLAB)),
         ],
         input_output_aliases=aliases,
-        compiler_params=pltpu.CompilerParams(vmem_limit_bytes=22 * 2**20),
-        cost_estimate=HEAVY,
+        compiler_params=pltpu.CompilerParams(vmem_limit_bytes=20 * 2**20),
+        cost_estimate=cost,
     )(*operands)
 
 
@@ -277,12 +295,6 @@
 Z_FAR_BY = moves(
     lambda x, y, z, c: (x, y, z + 1, 1 - c) if c == half((z - 1) % 4) else None
 )
-FAR_FIRST = moves(
-    lambda x, y, z, c: (1 - x, y, z, c) if c != half(z) else (x, 1 - y, z, c)
-)
-FAR_SECOND = moves(
-    lambda x, y, z, c: (x, 1 - y, z, c) if c != half(z) else (1 - x, y, z, c)
-)
 Z_1 = moves(lambda x, y, z, c: (x, y, z ^ 1, c))
 Z_2 = moves(lambda x, y, z, c: (x, y, z ^ 2, c))
 
@@ -313,7 +325,7 @@
     mine = stack(raw1, raw2, raw3)
     other = send("other", mine, CORE)
     token, odd_b = after(token, odd_b)
-    odd_b1, far_b = send("odd_b1", odd_b, FIRST), send("far_b", odd_b, Z_FAR_BY)
+    odd_b1, far_b = send("odd_b1", odd_b, SECOND), send("far_b", odd_b, Z_FAR_BY)
     token, odd_t1 = after(token, odd_t1, cost=HEAVY)
     odd_t3 = send("odd_t3", odd_t1, SECOND)
     product, token = mul(
@@ -328,60 +340,61 @@
     )
     plane, total = plane_rows(mine, other, total, token)
     far = choose(total, far_t, far_b)
-    far1, far2 = send("far1", far, FAR_FIRST), send("far2", far, FAR_SECOND)
+    far1, far2 = send("far1", far, SECOND), send("far2", far, FIRST)
     total_1 = send("total_1", total, Z_1)
     token, odd_b1 = after(total, odd_b1)
     token, odd_b = after(token, odd_b)
-    odd_b2 = send("odd_b2", odd_b, SECOND)
+    odd_b2 = send("odd_b2", odd_b, FIRST)
     token, total, total_1 = after(token, total, total_1)
+    token, odd_t3 = after(token, odd_t3)
     product, total = mul(
         left,
         [
             [(odd_t3, 0, 1, "both", 0)],
             [(odd_b, 0, 1, "here", 1)],
-            [(odd_b1, 0, 1, "first", 1)],
+            [(odd_b1, 0, 1, "second", 1)],
         ],
         product,
         sums=(total, total_1),
     )
     total_2 = send("total_2", total, Z_2)
-    token, total_2 = after(total, total_2)
-    token, far1 = after(token, far1)
-    far3 = send("far3", far1, FAR_SECOND)
-    token, odd_b1 = after(token, odd_b1)
-    odd_b3 = send("odd_b3", odd_b1, SECOND)
+    far_o = send("far_o", far, CORE)
+    token, far1 = after(total, far1)
+    last = send("last", stack(far1, odd_b1), FIRST)
+    far1_o = send("far1_o", far1, CORE)
     token, odd_b2 = after(token, odd_b2)
     token, far2 = after(token, far2)
-    far_mine = stack(far, far1, far2)
-    far_other = send("far_other", far_mine, CORE)
+    far2_o = send("far2_o", far2, CORE)
     product, total = mul(
         left,
         [
-            [(top, 0, 0, "here", 0), (far_mine, 0, 0, "here", 0)],
-            [(bottom, 0, 0, "here", 1), (far_other, 0, 0, "here", 1)],
-            [(plane, 0, 0, "first", 0), (far_mine, 1, 0, "x", 0)],
-            [(plane, 1, 0, "first", 1), (far_other, 1, 0, "y", 1)],
-            [(plane, 2, 0, "second", 0), (far_mine, 2, 0, "y", 0)],
-            [(plane, 3, 0, "second", 1), (far_other, 2, 0, "x", 1)],
+            [(top, 0, 0, "here", 0), (far, 0, 0, "here", 0)],
+            [(bottom, 0, 0, "here", 1), (far_o, 0, 0, "here", 1)],
+            [(plane, 0, 0, "first", 0), (far1, 0, 0, "second", 0)],
+            [(plane, 1, 0, "first", 1), (far1_o, 0, 0, "first", 1)],
+            [(plane, 2, 0, "second", 0), (far2, 0, 0, "first", 0)],
+            [(plane, 3, 0, "second", 1), (far2_o, 0, 0, "second", 1)],
+            [(odd_b2, 0, 1, "first", 1)],
         ],
         product,
         sums=(total, total_2),
-    )
-    occupation = total[0, 0] / (n * math.sqrt(DEPTH))
-    token, odd_b3 = after(total, odd_b3)
-    token, far3 = after(token, far3)
-    far3_other = send("far3_other", far3, CORE)
+        cost=LIGHT,
+    )
+    occupation = scaled(total, 1.0 / (n * math.sqrt(DEPTH)))
+    token, last = after(total, last)
+    last_o = send("last_o", last, CORE)
     product, token = mul(
         left,
         [
-            [(odd_b2, 0, 1, "second", 1)],
-            [(odd_b3, 0, 1, "both", 1)],
-            [(plane, 4, 0, "both", 0), (far3, 0, 0, "both", 0)],
-            [(plane, 5, 0, "both", 1), (far3_other, 0, 0, "both", 1)],
+            [(last, 1, 1, "both", 1)],
+            [(plane, 4, 0, "both", 0), (last, 0, 0, "both", 0)],
         ],
         product,
     )
-    return product, jnp.reshape(occupation, (1,))
+    product, token = mul(
+        left, [[(plane, 5, 0, "both", 1), (last_o, 0, 0, "both", 1)]], product
+    )
+    return product, occupation
 
 
 def on_any(n, density):

time: 91.6 us -> 89.1 us (0.973)
  waiting for transfers between devices: 30.3 us -> 20.3 us
  starting transfers between devices: 30.4 us -> 37.5 us
  Pallas kernels: 26.1 us -> 29.2 us
  between operations: 2.54 us -> 0.84 us
    ppermute x22 -> x23, waiting for transfers between devices: 30.3 us -> 20.3 us  [send(): return lax.ppermute(a, BOTH, pairs)]
    ppermute x22 -> x23, starting transfers between devices: 30.4 us -> 37.5 us  [send(): return lax.ppermute(a, BOTH, pairs)]
    pallas_call x4 -> x5, Pallas kernels: 22.5 us -> 24.1 us  [multiply(): pl.pallas_call(functools.partial(multiply_kernel, listed, len(arrays), pr...]
    pallas_call x15 -> x13, Pallas kernels: 1.81 us -> 2.74 us  [after(): pl.pallas_call(after_kernel, out_shape=(like(8, 128), *(like(*a.shape) fo...]
  transfers between devices with their start and end apart: 22 -> 23, of which waited for: 10 -> 7; matrix products, arithmetic and copies ran while one was open for 1% -> 0% of each run, Pallas kernels for 21% -> 29%
where the time goes in v3:
time: 89.1 us; the launch traced here: 88.9 us
  starting transfers between devices  37.5 us (42%)
  Pallas kernels  29.2 us (33%)
  waiting for transfers between devices  20.3 us (23%)
  local copies, waits for them, and re-layouts  1.08 us (1%)
    ppermute x23, starting transfers between devices, send(): return lax.ppermute(a, BOTH, pairs)  37.5 us
    pallas_call x5, Pallas kernels, multiply(): pl.pallas_call(functools.partial(multiply_kernel, listed, len(arrays), pr...  24.1 us
    ppermute x23, waiting for transfers between devices, send(): return lax.ppermute(a, BOTH, pairs)  20.3 us
    pallas_call x13, Pallas kernels, after(): pl.pallas_call(after_kernel, out_shape=(like(8, 128), *(like(*a.shape) fo...  2.74 us
    pallas_call x5, Pallas kernels, in_vmem(): pl.pallas_call(kernel, out_shape=out_shape, in_specs=[VMEM] * len(arrays)...  1.84 us
  transfers between devices with their start and end apart: 23, of which 7 were waited for; matrix products, arithmetic and copies ran while one was open for 0% of the time, Pallas kernels for 29%

profile of v3, /device:TPU:1, one launch (start us, length us, event | category | flops | bytes accessed | tf_op | source)
XLA Modules:
  0.0 88.9 jit_solution(9467996379245057686)
XLA Ops:
  0.6 1.1 %slice.3.mine = f32[1024,128]{1,0:T(8,128)S(1)} slice(f32[1024,8192]{1,0:T(8,128)} %param.1), slice={[0:1024], [0:128]} | slice | bytes 1048576 | tf_op jit(solution)/shard_map/slice | solution.py:312
  1.7 0.1 collective-permute-start
  1.8 2.7 %collective-permute-start.1 = (f32[1024,128]{1,0:T(8,128)S(1)}, f32[1024,128]{1,0:T(8,128)S(1)}, u32[]{:S(2)}, u32[]{:S(2)}) collective-permute-start(f32[1024,128]{1,0:T(8,128)S(1)} %slice.3.mine), channel_id=1, source_target_pairs={{0,2},{1,5},{2,0},{3,7},{4,6},{5,1},{6,4},{7,3},{8,10},{9,13},{10,... | collective-permute-start | bytes 1572872 | tf_op jit(solution)/shard_map/raw1/ppermute | solution.py:304
  4.5 0.9 shard_map.30
  5.4 1.9 %collective-permute-start.2 = (f32[512,256]{1,0:T(8,128)S(1)}, f32[512,256]{1,0:T(8,128)S(1)}, u32[]{:S(2)}, u32[]{:S(2)}) collective-permute-start(f32[512,256]{1,0:T(8,128)S(1)} %get-tuple-element.46.refs_1_), channel_id=1, source_target_pairs={{0,24},{1,8},{2,26},{3,10},{4,28},{5,12},{6,30},{7,14},{8,0},{9,16... | collective-permute-start | bytes 1572872 | tf_op jit(solution)/shard_map/odd_t/ppermute | solution.py:304
  7.3 1.2 %collective-permute-start.3 = (f32[1024,128]{1,0:T(8,128)S(1)}, f32[1024,128]{1,0:T(8,128)S(1)}, u32[]{:S(2)}, u32[]{:S(2)}) collective-permute-start(f32[1024,128]{1,0:T(8,128)S(1)} %get-tuple-element.48), channel_id=1, source_target_pairs={{0,4},{1,3},{2,6},{3,1},{4,0},{5,7},{6,2},{7,5},{8,12},{9,11},{10,... | collective-permute-start | bytes 1572872 | tf_op jit(solution)/shard_map/raw2/ppermute | solution.py:304
  8.5 2.9 %collective-permute-done.1.refs_0_ = f32[1024,128]{1,0:T(8,128)S(1)} collective-permute-done((f32[1024,128]{1,0:T(8,128)S(1)}, f32[1024,128]{1,0:T(8,128)S(1)}, u32[]{:S(2)}, u32[]{:S(2)}) %collective-permute-start.1) | collective-permute-done | bytes 524320 | tf_op jit(solution)/shard_map/raw1/ppermute | solution.py:304
  11.4 0.1 shard_map.31
  11.5 1.5 %collective-permute-start.4 = (f32[1024,128]{1,0:T(8,128)S(1)}, f32[1024,128]{1,0:T(8,128)S(1)}, u32[]{:S(2)}, u32[]{:S(2)}) collective-permute-start(f32[1024,128]{1,0:T(8,128)S(1)} %get-tuple-element.44.refs_0_), channel_id=1, source_target_pairs={{0,4},{1,3},{2,6},{3,1},{4,0},{5,7},{6,2},{7,5},{8,12},{9,11},{10,... | collective-permute-start | bytes 1572872 | tf_op jit(solution)/shard_map/raw3/ppermute | solution.py:304
  13.0 4.5 %collective-permute-start.6 = (f32[512,256]{1,0:T(8,128)S(1)}, f32[512,256]{1,0:T(8,128)S(1)}, u32[]{:S(2)}, u32[]{:S(2)}) collective-permute-start(f32[512,256]{1,0:T(8,128)S(1)} %get-tuple-element.53.refs_3_), channel_id=1, source_target_pairs={{0,24},{1,8},{2,26},{3,10},{4,28},{5,12},{6,30},{7,14},{8,0},{9,16... | collective-permute-start | bytes 1572872 | tf_op jit(solution)/shard_map/odd_b/ppermute | solution.py:304
  17.4 3.1 %collective-permute-done.2.refs_0_ = f32[512,256]{1,0:T(8,128)S(1)} collective-permute-done((f32[512,256]{1,0:T(8,128)S(1)}, f32[512,256]{1,0:T(8,128)S(1)}, u32[]{:S(2)}, u32[]{:S(2)}) %collective-permute-start.2) | collective-permute-done | bytes 524320 | tf_op jit(solution)/shard_map/odd_t/ppermute | solution.py:304
  20.6 0.1 shard_map.32
  20.6 1.3 %collective-permute-start.7 = (f32[512,256]{1,0:T(8,128)S(1)}, f32[512,256]{1,0:T(8,128)S(1)}, u32[]{:S(2)}, u32[]{:S(2)}) collective-permute-start(f32[512,256]{1,0:T(8,128)S(1)} %get-tuple-element.51.refs_1_), channel_id=1, source_target_pairs={{0,2},{1,5},{2,0},{3,7},{4,6},{5,1},{6,4},{7,3},{8,10},{9,13},{10,... | collective-permute-start | bytes 1572872 | tf_op jit(solution)/shard_map/odd_t1/ppermute | solution.py:304
  21.9 1.2 %collective-permute-start.8 = (f32[512,256]{1,0:T(8,128)S(1)}, f32[512,256]{1,0:T(8,128)S(1)}, u32[]{:S(2)}, u32[]{:S(2)}) collective-permute-start(f32[512,256]{1,0:T(8,128)S(1)} %get-tuple-element.51.refs_1_), channel_id=1, source_target_pairs={{0,4},{1,3},{2,6},{3,1},{4,0},{5,7},{6,2},{7,5},{8,12},{9,11},{10,... | collective-permute-start | bytes 1572872 | tf_op jit(solution)/shard_map/odd_t2/ppermute | solution.py:304
  23.1 3.3 %collective-permute-start.9 = (f32[512,256]{1,0:T(8,128)S(1)}, f32[512,256]{1,0:T(8,128)S(1)}, u32[]{:S(2)}, u32[]{:S(2)}) collective-permute-start(f32[512,256]{1,0:T(8,128)S(1)} %get-tuple-element.51.refs_1_), channel_id=1, source_target_pairs={{1,9},{3,11},{5,13},{7,15},{8,16},{10,18},{12,20},{14,22},{16,24},... | collective-permute-start | bytes 1572872 | tf_op jit(solution)/shard_map/far_t/ppermute | solution.py:304
  26.5 0.1 shard_map.33
  26.6 4.9 %collective-permute-done.6.refs_0_ = f32[512,256]{1,0:T(8,128)S(1)} collective-permute-done((f32[512,256]{1,0:T(8,128)S(1)}, f32[512,256]{1,0:T(8,128)S(1)}, u32[]{:S(2)}, u32[]{:S(2)}) %collective-permute-start.6) | collective-permute-done | bytes 524320 | tf_op jit(solution)/shard_map/odd_b/ppermute | solution.py:304
  31.5 0.1 shard_map.35
  31.6 1.3 %collective-permute-start.10 = (f32[512,256]{1,0:T(8,128)S(1)}, f32[512,256]{1,0:T(8,128)S(1)}, u32[]{:S(2)}, u32[]{:S(2)}) collective-permute-start(f32[512,256]{1,0:T(8,128)S(1)} %get-tuple-element.60.refs_0_), channel_id=1, source_target_pairs={{1,8},{3,10},{5,12},{7,14},{8,17},{10,19},{12,21},{14,23},{16,25},... | collective-permute-start | bytes 1572872 | tf_op jit(solution)/shard_map/far_b/ppermute | solution.py:304
  32.9 1.5 %collective-permute-start.12 = (f32[512,256]{1,0:T(8,128)S(1)}, f32[512,256]{1,0:T(8,128)S(1)}, u32[]{:S(2)}, u32[]{:S(2)}) collective-permute-start(f32[512,256]{1,0:T(8,128)S(1)} %get-tuple-element.60.refs_0_), channel_id=1, source_target_pairs={{0,4},{1,3},{2,6},{3,1},{4,0},{5,7},{6,2},{7,5},{8,12},{9,11},{10,... | collective-permute-start | bytes 1572872 | tf_op jit(solution)/shard_map/odd_b1/ppermute | solution.py:304
  34.4 0.1 shard_map.34.mine
  34.5 1.7 %collective-permute-start.5 = (f32[3072,128]{1,0:T(8,128)S(1)}, f32[3072,128]{1,0:T(8,128)S(1)}, u32[]{:S(2)}, u32[]{:S(2)}) collective-permute-start(f32[3072,128]{1,0:T(8,128)S(1)} %shard_map.34.mine), channel_id=1, source_target_pairs={{0,1},{1,0},{2,3},{3,2},{4,5},{5,4},{6,7},{7,6},{8,9},{9,8},{10,11... | collective-permute-start | bytes 4718600 | tf_op jit(solution)/shard_map/other/ppermute | solution.py:304
  36.4 1.3 %collective-permute-start.14 = (f32[512,256]{1,0:T(8,128)S(1)}, f32[512,256]{1,0:T(8,128)S(1)}, u32[]{:S(2)}, u32[]{:S(2)}) collective-permute-start(f32[512,256]{1,0:T(8,128)S(1)} %get-tuple-element.55.refs_2_), channel_id=1, source_target_pairs={{0,4},{1,3},{2,6},{3,1},{4,0},{5,7},{6,2},{7,5},{8,12},{9,11},{10,... | collective-permute-start | bytes 1572872 | tf_op jit(solution)/shard_map/odd_t3/ppermute | solution.py:304
  37.6 4.3 %shard_map.37 = (f32[1024,8192]{1,0:T(8,128)}, f32[8,128]{1,0:T(8,128)S(1)}) custom-call(bf16[1024,768]{1,0:T(8,128)(2,1)S(1)} %get-tuple-element.42.refs_0_, f32[512,256]{1,0:T(8,128)S(1)} %get-tuple-element.51.refs_1_, f32[512,256]{1,0:T(8,128)S(1)} %get-tuple-element.55.refs_2_, f32[512,256]{1,0:T(8,128)S(1)} %collective-permute-done.8.refs_3_, ...), custom_call_target="tpu_custom_call" | custom-call | flops 10000000000 | bytes 100000000 | tf_op jit(solution)/shard_map/pallas_call | solution.py:247
  42.0 0.8 shard_map.38
  42.8 2.0 %collective-permute-start.13 = (f32[8,128]{1,0:T(8,128)S(1)}, f32[8,128]{1,0:T(8,128)S(1)}, u32[]{:S(2)}, u32[]{:S(2)}) collective-permute-start(f32[8,128]{1,0:T(8,128)S(1)} %get-tuple-element.59.token.refs_0_), channel_id=1, source_target_pairs={{0,8},{1,9},{2,10},{3,11},{4,12},{5,13},{6,14},{7,15},{8,0},{9,1},... | collective-permute-start | bytes 12296 | tf_op jit(solution)/shard_map/total_1/ppermute | solution.py:304
  44.8 0.3 collective-permute-start.15
  45.1 0.5 collective-permute-start.18
  45.8 0.1 shard_map.41
  45.8 1.0 %collective-permute-start.17 = (f32[512,256]{1,0:T(8,128)S(1)}, f32[512,256]{1,0:T(8,128)S(1)}, u32[]{:S(2)}, u32[]{:S(2)}) collective-permute-start(f32[512,256]{1,0:T(8,128)S(1)} %get-tuple-element.65.refs_2_), channel_id=1, source_target_pairs={{0,2},{1,5},{2,0},{3,7},{4,6},{5,1},{6,4},{7,3},{8,10},{9,13},{10,... | collective-permute-start | bytes 1572872 | tf_op jit(solution)/shard_map/odd_b2/ppermute | solution.py:304
  46.8 0.3 collective-permute-done.14.refs_0_
  47.1 0.7 shard_map.43
  47.8 4.4 %shard_map.44 = (f32[1024,8192]{1,0:T(8,128)}, f32[8,128]{1,0:T(8,128)S(1)}) custom-call(bf16[1024,768]{1,0:T(8,128)(2,1)S(1)} %get-tuple-element.42.refs_0_, f32[512,256]{1,0:T(8,128)S(1)} %get-tuple-element.64.refs_1_, f32[512,256]{1,0:T(8,128)S(1)} %get-tuple-element.65.refs_2_, ...), custom_call_target="tpu_custom_call", output_to_operand_aliasing={{0}: (4, {})} | custom-call | flops 10000000000 | bytes 100000000 | tf_op jit(solution)/shard_map/pallas_call | solution.py:247
  52.1 4.4 %collective-permute-done.15.refs_0_ = f32[512,256]{1,0:T(8,128)S(1)} collective-permute-done((f32[512,256]{1,0:T(8,128)S(1)}, f32[512,256]{1,0:T(8,128)S(1)}, u32[]{:S(2)}, u32[]{:S(2)}) %collective-permute-start.15) | collective-permute-done | bytes 524320 | tf_op jit(solution)/shard_map/far1/ppermute | solution.py:304
  56.5 0.1 shard_map.45
  56.6 0.1 shard_map.49
  56.6 0.5 collective-permute-start.21
  57.1 7.4 %collective-permute-start.11 = (f32[512,256]{1,0:T(8,128)S(1)}, f32[512,256]{1,0:T(8,128)S(1)}, u32[]{:S(2)}, u32[]{:S(2)}) collective-permute-start(f32[512,256]{1,0:T(8,128)S(1)} %shard_map.39.refs_2_), channel_id=1, source_target_pairs={{0,1},{1,0},{2,3},{3,2},{4,5},{5,4},{6,7},{7,6},{8,9},{9,8},{10,11... | collective-permute-start | bytes 1572872 | tf_op jit(solution)/shard_map/far_o/ppermute | solution.py:304
  64.6 1.9 %collective-permute-done.17.refs_0_ = f32[512,256]{1,0:T(8,128)S(1)} collective-permute-done((f32[512,256]{1,0:T(8,128)S(1)}, f32[512,256]{1,0:T(8,128)S(1)}, u32[]{:S(2)}, u32[]{:S(2)}) %collective-permute-start.17) | collective-permute-done | bytes 524320 | tf_op jit(solution)/shard_map/odd_b2/ppermute | solution.py:304
  66.5 0.7 shard_map.47
  67.2 0.4 collective-permute-start.20
  67.6 2.9 %collective-permute-done.20.refs_13_ = f32[8,128]{1,0:T(8,128)S(1)} collective-permute-done((f32[8,128]{1,0:T(8,128)S(1)}, f32[8,128]{1,0:T(8,128)S(1)}, u32[]{:S(2)}, u32[]{:S(2)}) %collective-permute-start.20) | collective-permute-done | bytes 4128 | tf_op jit(solution)/shard_map/total_2/ppermute | solution.py:304
  70.5 8.9 %shard_map.48 = (f32[1024,8192]{1,0:T(8,128)}, f32[8,128]{1,0:T(8,128)S(1)}) custom-call(bf16[1024,768]{1,0:T(8,128)(2,1)S(1)} %get-tuple-element.42.refs_0_, f32[512,256]{1,0:T(8,128)S(1)} %get-tuple-element.46.refs_1_, f32[512,256]{1,0:T(8,128)S(1)} %shard_map.39.refs_2_, ...), custom_call_target="tpu_custom_call", output_to_operand_aliasing={{0}: (11, {})} | custom-call | flops 1 | bytes 1 | tf_op jit(solution)/shard_map/pallas_call | solution.py:247
  79.4 0.7 shard_map.50
  80.2 1.7 %collective-permute-start.22 = (f32[1024,256]{1,0:T(8,128)S(1)}, f32[1024,256]{1,0:T(8,128)S(1)}, u32[]{:S(2)}, u32[]{:S(2)}) collective-permute-start(f32[1024,256]{1,0:T(8,128)S(1)} %get-tuple-element.78.refs_1_), channel_id=1, source_target_pairs={{0,1},{1,0},{2,3},{3,2},{4,5},{5,4},{6,7},{7,6},{8,9},{9,8},{10,11... | collective-permute-start | bytes 3145736 | tf_op jit(solution)/shard_map/last_o/ppermute | solution.py:304
  81.8 0.6 shard_map.53
  82.4 3.8 %shard_map.51 = (f32[1024,8192]{1,0:T(8,128)}, f32[8,128]{1,0:T(8,128)}) custom-call(bf16[1024,768]{1,0:T(8,128)(2,1)S(1)} %get-tuple-element.42.refs_0_, f32[1024,256]{1,0:T(8,128)S(1)} %get-tuple-element.78.refs_1_, f32[3072,256]{1,0:T(8,128)S(1)} %get-tuple-element.58.refs_5_.refs_2_.refs_1_, ...), custom_call_target="tpu_custom_call", output_to_operand_aliasing={{0}: (3, {})} | custom-call | flops 10000000000 | bytes 100000000 | tf_op jit(solution)/shard_map/pallas_call | solution.py:247
  86.2 2.7 %shard_map.52 = (f32[1024,8192]{1,0:T(8,128)}, f32[8,128]{1,0:T(8,128)}) custom-call(bf16[1024,768]{1,0:T(8,128)(2,1)S(1)} %get-tuple-element.42.refs_0_, f32[3072,256]{1,0:T(8,128)S(1)} %get-tuple-element.58.refs_5_.refs_2_.refs_1_, f32[1024,256]{1,0:T(8,128)S(1)} %collective-permute-done.22.refs_2_, ...), custom_call_target="tpu_custom_call", output_to_operand_aliasing={{0}: (3, {})} | custom-call | flops 10000000000 | bytes 100000000 | tf_op jit(solution)/shard_map/pallas_call | solution.py:247
  (23 shorter events, 0.3 us)
Async XLA Ops:
  1.7 2.8 %collective-permute-start = (f32[1024,128]{1,0:T(8,128)S(1)}, f32[1024,128]{1,0:T(8,128)S(1)}, u32[]{:S(2)}, u32[]{:S(2)}) collective-permute-start(f32[1024,128]{1,0:T(8,128)S(1)} %slice.3.mine), channel_id=1, source_target_pairs={{0,1},{1,0},{2,3},{3,2},{4,5},{5,4},{6,7},{7,6},{8,9},{9,8},{10,11... | collective-permute-start | bytes 1572872 | tf_op jit(solution)/shard_map/sib/ppermute | solution.py:304
  1.8 9.6 %collective-permute-start.1 = (f32[1024,128]{1,0:T(8,128)S(1)}, f32[1024,128]{1,0:T(8,128)S(1)}, u32[]{:S(2)}, u32[]{:S(2)}) collective-permute-start(f32[1024,128]{1,0:T(8,128)S(1)} %slice.3.mine), channel_id=1, source_target_pairs={{0,2},{1,5},{2,0},{3,7},{4,6},{5,1},{6,4},{7,3},{8,10},{9,13},{10,... | collective-permute-start | bytes 1572872 | tf_op jit(solution)/shard_map/raw1/ppermute | solution.py:304
  5.4 15.2 %collective-permute-start.2 = (f32[512,256]{1,0:T(8,128)S(1)}, f32[512,256]{1,0:T(8,128)S(1)}, u32[]{:S(2)}, u32[]{:S(2)}) collective-permute-start(f32[512,256]{1,0:T(8,128)S(1)} %get-tuple-element.46.refs_1_), channel_id=1, source_target_pairs={{0,24},{1,8},{2,26},{3,10},{4,28},{5,12},{6,30},{7,14},{8,0},{9,16... | collective-permute-start | bytes 1572872 | tf_op jit(solution)/shard_map/odd_t/ppermute | solution.py:304
  7.3 15.8 %collective-permute-start.3 = (f32[1024,128]{1,0:T(8,128)S(1)}, f32[1024,128]{1,0:T(8,128)S(1)}, u32[]{:S(2)}, u32[]{:S(2)}) collective-permute-start(f32[1024,128]{1,0:T(8,128)S(1)} %get-tuple-element.48), channel_id=1, source_target_pairs={{0,4},{1,3},{2,6},{3,1},{4,0},{5,7},{6,2},{7,5},{8,12},{9,11},{10,... | collective-permute-start | bytes 1572872 | tf_op jit(solution)/shard_map/raw2/ppermute | solution.py:304
  11.5 15.0 %collective-permute-start.4 = (f32[1024,128]{1,0:T(8,128)S(1)}, f32[1024,128]{1,0:T(8,128)S(1)}, u32[]{:S(2)}, u32[]{:S(2)}) collective-permute-start(f32[1024,128]{1,0:T(8,128)S(1)} %get-tuple-element.44.refs_0_), channel_id=1, source_target_pairs={{0,4},{1,3},{2,6},{3,1},{4,0},{5,7},{6,2},{7,5},{8,12},{9,11},{10,... | collective-permute-start | bytes 1572872 | tf_op jit(solution)/shard_map/raw3/ppermute | solution.py:304
  13.0 18.5 %collective-permute-start.6 = (f32[512,256]{1,0:T(8,128)S(1)}, f32[512,256]{1,0:T(8,128)S(1)}, u32[]{:S(2)}, u32[]{:S(2)}) collective-permute-start(f32[512,256]{1,0:T(8,128)S(1)} %get-tuple-element.53.refs_3_), channel_id=1, source_target_pairs={{0,24},{1,8},{2,26},{3,10},{4,28},{5,12},{6,30},{7,14},{8,0},{9,16... | collective-permute-start | bytes 1572872 | tf_op jit(solution)/shard_map/odd_b/ppermute | solution.py:304
  20.6 13.9 %collective-permute-start.7 = (f32[512,256]{1,0:T(8,128)S(1)}, f32[512,256]{1,0:T(8,128)S(1)}, u32[]{:S(2)}, u32[]{:S(2)}) collective-permute-start(f32[512,256]{1,0:T(8,128)S(1)} %get-tuple-element.51.refs_1_), channel_id=1, source_target_pairs={{0,2},{1,5},{2,0},{3,7},{4,6},{5,1},{6,4},{7,3},{8,10},{9,13},{10,... | collective-permute-start | bytes 1572872 | tf_op jit(solution)/shard_map/odd_t1/ppermute | solution.py:304
  21.9 14.4 %collective-permute-start.8 = (f32[512,256]{1,0:T(8,128)S(1)}, f32[512,256]{1,0:T(8,128)S(1)}, u32[]{:S(2)}, u32[]{:S(2)}) collective-permute-start(f32[512,256]{1,0:T(8,128)S(1)} %get-tuple-element.51.refs_1_), channel_id=1, source_target_pairs={{0,4},{1,3},{2,6},{3,1},{4,0},{5,7},{6,2},{7,5},{8,12},{9,11},{10,... | collective-permute-start | bytes 1572872 | tf_op jit(solution)/shard_map/odd_t2/ppermute | solution.py:304
  23.1 21.6 %collective-permute-start.9 = (f32[512,256]{1,0:T(8,128)S(1)}, f32[512,256]{1,0:T(8,128)S(1)}, u32[]{:S(2)}, u32[]{:S(2)}) collective-permute-start(f32[512,256]{1,0:T(8,128)S(1)} %get-tuple-element.51.refs_1_), channel_id=1, source_target_pairs={{1,9},{3,11},{5,13},{7,15},{8,16},{10,18},{12,20},{14,22},{16,24},... | collective-permute-start | bytes 1572872 | tf_op jit(solution)/shard_map/far_t/ppermute | solution.py:304
  31.6 13.2 %collective-permute-start.10 = (f32[512,256]{1,0:T(8,128)S(1)}, f32[512,256]{1,0:T(8,128)S(1)}, u32[]{:S(2)}, u32[]{:S(2)}) collective-permute-start(f32[512,256]{1,0:T(8,128)S(1)} %get-tuple-element.60.refs_0_), channel_id=1, source_target_pairs={{1,8},{3,10},{5,12},{7,14},{8,17},{10,19},{12,21},{14,23},{16,25},... | collective-permute-start | bytes 1572872 | tf_op jit(solution)/shard_map/far_b/ppermute | solution.py:304
  32.9 12.8 %collective-permute-start.12 = (f32[512,256]{1,0:T(8,128)S(1)}, f32[512,256]{1,0:T(8,128)S(1)}, u32[]{:S(2)}, u32[]{:S(2)}) collective-permute-start(f32[512,256]{1,0:T(8,128)S(1)} %get-tuple-element.60.refs_0_), channel_id=1, source_target_pairs={{0,4},{1,3},{2,6},{3,1},{4,0},{5,7},{6,2},{7,5},{8,12},{9,11},{10,... | collective-permute-start | bytes 1572872 | tf_op jit(solution)/shard_map/odd_b1/ppermute | solution.py:304
  34.5 7.5 %collective-permute-start.5 = (f32[3072,128]{1,0:T(8,128)S(1)}, f32[3072,128]{1,0:T(8,128)S(1)}, u32[]{:S(2)}, u32[]{:S(2)}) collective-permute-start(f32[3072,128]{1,0:T(8,128)S(1)} %shard_map.34.mine), channel_id=1, source_target_pairs={{0,1},{1,0},{2,3},{3,2},{4,5},{5,4},{6,7},{7,6},{8,9},{9,8},{10,11... | collective-permute-start | bytes 4718600 | tf_op jit(solution)/shard_map/other/ppermute | solution.py:304
  36.4 10.7 %collective-permute-start.14 = (f32[512,256]{1,0:T(8,128)S(1)}, f32[512,256]{1,0:T(8,128)S(1)}, u32[]{:S(2)}, u32[]{:S(2)}) collective-permute-start(f32[512,256]{1,0:T(8,128)S(1)} %get-tuple-element.55.refs_2_), channel_id=1, source_target_pairs={{0,4},{1,3},{2,6},{3,1},{4,0},{5,7},{6,2},{7,5},{8,12},{9,11},{10,... | collective-permute-start | bytes 1572872 | tf_op jit(solution)/shard_map/odd_t3/ppermute | solution.py:304
  42.8 4.1 %collective-permute-start.13 = (f32[8,128]{1,0:T(8,128)S(1)}, f32[8,128]{1,0:T(8,128)S(1)}, u32[]{:S(2)}, u32[]{:S(2)}) collective-permute-start(f32[8,128]{1,0:T(8,128)S(1)} %get-tuple-element.59.token.refs_0_), channel_id=1, source_target_pairs={{0,8},{1,9},{2,10},{3,11},{4,12},{5,13},{6,14},{7,15},{8,0},{9,1},... | collective-permute-start | bytes 12296 | tf_op jit(solution)/shard_map/total_1/ppermute | solution.py:304
  44.8 11.7 %collective-permute-start.15 = (f32[512,256]{1,0:T(8,128)S(1)}, f32[512,256]{1,0:T(8,128)S(1)}, u32[]{:S(2)}, u32[]{:S(2)}) collective-permute-start(f32[512,256]{1,0:T(8,128)S(1)} %shard_map.39.refs_2_), channel_id=1, source_target_pairs={{0,4},{1,3},{2,6},{3,1},{4,0},{5,7},{6,2},{7,5},{8,12},{9,11},{10,... | collective-permute-start | bytes 1572872 | tf_op jit(solution)/shard_map/far1/ppermute | solution.py:304
  45.1 21.4 %collective-permute-start.18 = (f32[512,256]{1,0:T(8,128)S(1)}, f32[512,256]{1,0:T(8,128)S(1)}, u32[]{:S(2)}, u32[]{:S(2)}) collective-permute-start(f32[512,256]{1,0:T(8,128)S(1)} %shard_map.39.refs_2_), channel_id=1, source_target_pairs={{0,2},{1,5},{2,0},{3,7},{4,6},{5,1},{6,4},{7,3},{8,10},{9,13},{10,... | collective-permute-start | bytes 1572872 | tf_op jit(solution)/shard_map/far2/ppermute | solution.py:304
  45.8 20.6 %collective-permute-start.17 = (f32[512,256]{1,0:T(8,128)S(1)}, f32[512,256]{1,0:T(8,128)S(1)}, u32[]{:S(2)}, u32[]{:S(2)}) collective-permute-start(f32[512,256]{1,0:T(8,128)S(1)} %get-tuple-element.65.refs_2_), channel_id=1, source_target_pairs={{0,2},{1,5},{2,0},{3,7},{4,6},{5,1},{6,4},{7,3},{8,10},{9,13},{10,... | collective-permute-start | bytes 1572872 | tf_op jit(solution)/shard_map/odd_b2/ppermute | solution.py:304
  56.6 22.8 %collective-permute-start.21 = (f32[1024,256]{1,0:T(8,128)S(1)}, f32[1024,256]{1,0:T(8,128)S(1)}, u32[]{:S(2)}, u32[]{:S(2)}) collective-permute-start(f32[1024,256]{1,0:T(8,128)S(1)} %shard_map.49), channel_id=1, source_target_pairs={{0,2},{1,5},{2,0},{3,7},{4,6},{5,1},{6,4},{7,3},{8,10},{9,13},{10,... | collective-permute-start | bytes 3145736 | tf_op jit(solution)/shard_map/last/ppermute | solution.py:304
  57.1 13.4 %collective-permute-start.11 = (f32[512,256]{1,0:T(8,128)S(1)}, f32[512,256]{1,0:T(8,128)S(1)}, u32[]{:S(2)}, u32[]{:S(2)}) collective-permute-start(f32[512,256]{1,0:T(8,128)S(1)} %shard_map.39.refs_2_), channel_id=1, source_target_pairs={{0,1},{1,0},{2,3},{3,2},{4,5},{5,4},{6,7},{7,6},{8,9},{9,8},{10,11... | collective-permute-start | bytes 1572872 | tf_op jit(solution)/shard_map/far_o/ppermute | solution.py:304
  64.5 6.0 %collective-permute-start.16 = (f32[512,256]{1,0:T(8,128)S(1)}, f32[512,256]{1,0:T(8,128)S(1)}, u32[]{:S(2)}, u32[]{:S(2)}) collective-permute-start(f32[512,256]{1,0:T(8,128)S(1)} %get-tuple-element.71.refs_6_.refs_0_), channel_id=1, source_target_pairs={{0,1},{1,0},{2,3},{3,2},{4,5},{5,4},{6,7},{7,6},{8,9},{9,8},{10,11... | collective-permute-start | bytes 1572872 | tf_op jit(solution)/shard_map/far1_o/ppermute | solution.py:304
  67.2 3.4 %collective-permute-start.19 = (f32[512,256]{1,0:T(8,128)S(1)}, f32[512,256]{1,0:T(8,128)S(1)}, u32[]{:S(2)}, u32[]{:S(2)}) collective-permute-start(f32[512,256]{1,0:T(8,128)S(1)} %get-tuple-element.74.refs_8_), channel_id=1, source_target_pairs={{0,1},{1,0},{2,3},{3,2},{4,5},{5,4},{6,7},{7,6},{8,9},{9,8},{10,11... | collective-permute-start | bytes 1572872 | tf_op jit(solution)/shard_map/far2_o/ppermute | solution.py:304
  67.2 3.4 %collective-permute-start.20 = (f32[8,128]{1,0:T(8,128)S(1)}, f32[8,128]{1,0:T(8,128)S(1)}, u32[]{:S(2)}, u32[]{:S(2)}) collective-permute-start(f32[8,128]{1,0:T(8,128)S(1)} %get-tuple-element.70.token.refs_12_), channel_id=1, source_target_pairs={{0,16},{1,17},{2,18},{3,19},{4,20},{5,21},{6,22},{7,23},{8,24},{9,... | collective-permute-start | bytes 12296 | tf_op jit(solution)/shard_map/total_2/ppermute | solution.py:304
  80.2 6.0 %collective-permute-start.22 = (f32[1024,256]{1,0:T(8,128)S(1)}, f32[1024,256]{1,0:T(8,128)S(1)}, u32[]{:S(2)}, u32[]{:S(2)}) collective-permute-start(f32[1024,256]{1,0:T(8,128)S(1)} %get-tuple-element.78.refs_1_), channel_id=1, source_target_pairs={{0,1},{1,0},{2,3},{3,2},{4,5},{5,4},{6,7},{7,6},{8,9},{9,8},{10,11... | collective-permute-start | bytes 3145736 | tf_op jit(solution)/shard_map/last_o/ppermute | solution.py:304

commit v4 on v3

--- a/solution.py
+++ b/solution.py
@@ -17,7 +17,7 @@
 
 VMEM = pl.BlockSpec(memory_space=pltpu.VMEM)
 ANY = pl.BlockSpec(memory_space=pl.ANY)
-SLAB = 512
+SLAB = 256
 LIGHT = pl.CostEstimate(flops=1, bytes_accessed=1, transcendentals=0)
 HEAVY = pl.CostEstimate(flops=10**10, bytes_accessed=10**8, transcendentals=0)
 

time: 89.1 us -> 88.8 us (level)
  no operation moved by 1% of the time
where the time goes in v4:
time: 88.8 us; the launch traced here: 88.6 us
  starting transfers between devices  37.8 us (43%)
  Pallas kernels  28.6 us (32%)
  waiting for transfers between devices  20.2 us (23%)
  local copies, waits for them, and re-layouts  1.08 us (1%)
    ppermute x23, starting transfers between devices, send(): return lax.ppermute(a, BOTH, pairs)  37.8 us
    pallas_call x5, Pallas kernels, multiply(): pl.pallas_call(functools.partial(multiply_kernel, listed, len(arrays), pr...  23.5 us
    ppermute x23, waiting for transfers between devices, send(): return lax.ppermute(a, BOTH, pairs)  20.2 us
    pallas_call x13, Pallas kernels, after(): pl.pallas_call(after_kernel, out_shape=(like(8, 128), *(like(*a.shape) fo...  2.74 us
    pallas_call x5, Pallas kernels, in_vmem(): pl.pallas_call(kernel, out_shape=out_shape, in_specs=[VMEM] * len(arrays)...  1.84 us
  transfers between devices with their start and end apart: 23, of which 7 were waited for; matrix products, arithmetic and copies ran while one was open for 0% of the time, Pallas kernels for 29%

profile of v4, /device:TPU:1, one launch (start us, length us, event | category | flops | bytes accessed | tf_op | source)
XLA Modules:
  0.0 88.6 jit_solution(11888262327571816739)
XLA Ops:
  0.6 1.1 %slice.3.mine = f32[1024,128]{1,0:T(8,128)S(1)} slice(f32[1024,8192]{1,0:T(8,128)} %param.1), slice={[0:1024], [0:128]} | slice | bytes 1048576 | tf_op jit(solution)/shard_map/slice | solution.py:312
  1.7 0.1 collective-permute-start
  1.8 2.7 %collective-permute-start.1 = (f32[1024,128]{1,0:T(8,128)S(1)}, f32[1024,128]{1,0:T(8,128)S(1)}, u32[]{:S(2)}, u32[]{:S(2)}) collective-permute-start(f32[1024,128]{1,0:T(8,128)S(1)} %slice.3.mine), channel_id=1, source_target_pairs={{0,2},{1,5},{2,0},{3,7},{4,6},{5,1},{6,4},{7,3},{8,10},{9,13},{10,... | collective-permute-start | bytes 1572872 | tf_op jit(solution)/shard_map/raw1/ppermute | solution.py:304
  4.5 0.9 shard_map.30
  5.4 1.9 %collective-permute-start.2 = (f32[512,256]{1,0:T(8,128)S(1)}, f32[512,256]{1,0:T(8,128)S(1)}, u32[]{:S(2)}, u32[]{:S(2)}) collective-permute-start(f32[512,256]{1,0:T(8,128)S(1)} %get-tuple-element.46.refs_1_), channel_id=1, source_target_pairs={{0,24},{1,8},{2,26},{3,10},{4,28},{5,12},{6,30},{7,14},{8,0},{9,16... | collective-permute-start | bytes 1572872 | tf_op jit(solution)/shard_map/odd_t/ppermute | solution.py:304
  7.3 1.2 %collective-permute-start.3 = (f32[1024,128]{1,0:T(8,128)S(1)}, f32[1024,128]{1,0:T(8,128)S(1)}, u32[]{:S(2)}, u32[]{:S(2)}) collective-permute-start(f32[1024,128]{1,0:T(8,128)S(1)} %get-tuple-element.48), channel_id=1, source_target_pairs={{0,4},{1,3},{2,6},{3,1},{4,0},{5,7},{6,2},{7,5},{8,12},{9,11},{10,... | collective-permute-start | bytes 1572872 | tf_op jit(solution)/shard_map/raw2/ppermute | solution.py:304
  8.5 2.9 %collective-permute-done.1.refs_0_ = f32[1024,128]{1,0:T(8,128)S(1)} collective-permute-done((f32[1024,128]{1,0:T(8,128)S(1)}, f32[1024,128]{1,0:T(8,128)S(1)}, u32[]{:S(2)}, u32[]{:S(2)}) %collective-permute-start.1) | collective-permute-done | bytes 524320 | tf_op jit(solution)/shard_map/raw1/ppermute | solution.py:304
  11.4 0.1 shard_map.31
  11.5 1.5 %collective-permute-start.4 = (f32[1024,128]{1,0:T(8,128)S(1)}, f32[1024,128]{1,0:T(8,128)S(1)}, u32[]{:S(2)}, u32[]{:S(2)}) collective-permute-start(f32[1024,128]{1,0:T(8,128)S(1)} %get-tuple-element.44.refs_0_), channel_id=1, source_target_pairs={{0,4},{1,3},{2,6},{3,1},{4,0},{5,7},{6,2},{7,5},{8,12},{9,11},{10,... | collective-permute-start | bytes 1572872 | tf_op jit(solution)/shard_map/raw3/ppermute | solution.py:304
  13.0 4.5 %collective-permute-start.6 = (f32[512,256]{1,0:T(8,128)S(1)}, f32[512,256]{1,0:T(8,128)S(1)}, u32[]{:S(2)}, u32[]{:S(2)}) collective-permute-start(f32[512,256]{1,0:T(8,128)S(1)} %get-tuple-element.53.refs_3_), channel_id=1, source_target_pairs={{0,24},{1,8},{2,26},{3,10},{4,28},{5,12},{6,30},{7,14},{8,0},{9,16... | collective-permute-start | bytes 1572872 | tf_op jit(solution)/shard_map/odd_b/ppermute | solution.py:304
  17.4 3.1 %collective-permute-done.2.refs_0_ = f32[512,256]{1,0:T(8,128)S(1)} collective-permute-done((f32[512,256]{1,0:T(8,128)S(1)}, f32[512,256]{1,0:T(8,128)S(1)}, u32[]{:S(2)}, u32[]{:S(2)}) %collective-permute-start.2) | collective-permute-done | bytes 524320 | tf_op jit(solution)/shard_map/odd_t/ppermute | solution.py:304
  20.6 0.1 shard_map.32
  20.6 1.3 %collective-permute-start.7 = (f32[512,256]{1,0:T(8,128)S(1)}, f32[512,256]{1,0:T(8,128)S(1)}, u32[]{:S(2)}, u32[]{:S(2)}) collective-permute-start(f32[512,256]{1,0:T(8,128)S(1)} %get-tuple-element.51.refs_1_), channel_id=1, source_target_pairs={{0,2},{1,5},{2,0},{3,7},{4,6},{5,1},{6,4},{7,3},{8,10},{9,13},{10,... | collective-permute-start | bytes 1572872 | tf_op jit(solution)/shard_map/odd_t1/ppermute | solution.py:304
  21.9 1.2 %collective-permute-start.8 = (f32[512,256]{1,0:T(8,128)S(1)}, f32[512,256]{1,0:T(8,128)S(1)}, u32[]{:S(2)}, u32[]{:S(2)}) collective-permute-start(f32[512,256]{1,0:T(8,128)S(1)} %get-tuple-element.51.refs_1_), channel_id=1, source_target_pairs={{0,4},{1,3},{2,6},{3,1},{4,0},{5,7},{6,2},{7,5},{8,12},{9,11},{10,... | collective-permute-start | bytes 1572872 | tf_op jit(solution)/shard_map/odd_t2/ppermute | solution.py:304
  23.1 3.3 %collective-permute-start.9 = (f32[512,256]{1,0:T(8,128)S(1)}, f32[512,256]{1,0:T(8,128)S(1)}, u32[]{:S(2)}, u32[]{:S(2)}) collective-permute-start(f32[512,256]{1,0:T(8,128)S(1)} %get-tuple-element.51.refs_1_), channel_id=1, source_target_pairs={{1,9},{3,11},{5,13},{7,15},{8,16},{10,18},{12,20},{14,22},{16,24},... | collective-permute-start | bytes 1572872 | tf_op jit(solution)/shard_map/far_t/ppermute | solution.py:304
  26.5 0.1 shard_map.33
  26.6 4.9 %collective-permute-done.6.refs_0_ = f32[512,256]{1,0:T(8,128)S(1)} collective-permute-done((f32[512,256]{1,0:T(8,128)S(1)}, f32[512,256]{1,0:T(8,128)S(1)}, u32[]{:S(2)}, u32[]{:S(2)}) %collective-permute-start.6) | collective-permute-done | bytes 524320 | tf_op jit(solution)/shard_map/odd_b/ppermute | solution.py:304
  31.5 0.1 shard_map.35
  31.6 1.3 %collective-permute-start.10 = (f32[512,256]{1,0:T(8,128)S(1)}, f32[512,256]{1,0:T(8,128)S(1)}, u32[]{:S(2)}, u32[]{:S(2)}) collective-permute-start(f32[512,256]{1,0:T(8,128)S(1)} %get-tuple-element.60.refs_0_), channel_id=1, source_target_pairs={{1,8},{3,10},{5,12},{7,14},{8,17},{10,19},{12,21},{14,23},{16,25},... | collective-permute-start | bytes 1572872 | tf_op jit(solution)/shard_map/far_b/ppermute | solution.py:304
  32.9 1.5 %collective-permute-start.12 = (f32[512,256]{1,0:T(8,128)S(1)}, f32[512,256]{1,0:T(8,128)S(1)}, u32[]{:S(2)}, u32[]{:S(2)}) collective-permute-start(f32[512,256]{1,0:T(8,128)S(1)} %get-tuple-element.60.refs_0_), channel_id=1, source_target_pairs={{0,4},{1,3},{2,6},{3,1},{4,0},{5,7},{6,2},{7,5},{8,12},{9,11},{10,... | collective-permute-start | bytes 1572872 | tf_op jit(solution)/shard_map/odd_b1/ppermute | solution.py:304
  34.4 0.1 shard_map.34.mine
  34.5 1.7 %collective-permute-start.5 = (f32[3072,128]{1,0:T(8,128)S(1)}, f32[3072,128]{1,0:T(8,128)S(1)}, u32[]{:S(2)}, u32[]{:S(2)}) collective-permute-start(f32[3072,128]{1,0:T(8,128)S(1)} %shard_map.34.mine), channel_id=1, source_target_pairs={{0,1},{1,0},{2,3},{3,2},{4,5},{5,4},{6,7},{7,6},{8,9},{9,8},{10,11... | collective-permute-start | bytes 4718600 | tf_op jit(solution)/shard_map/other/ppermute | solution.py:304
  36.3 0.1 shard_map.36
  36.4 1.3 %collective-permute-start.14 = (f32[512,256]{1,0:T(8,128)S(1)}, f32[512,256]{1,0:T(8,128)S(1)}, u32[]{:S(2)}, u32[]{:S(2)}) collective-permute-start(f32[512,256]{1,0:T(8,128)S(1)} %get-tuple-element.55.refs_2_), channel_id=1, source_target_pairs={{0,4},{1,3},{2,6},{3,1},{4,0},{5,7},{6,2},{7,5},{8,12},{9,11},{10,... | collective-permute-start | bytes 1572872 | tf_op jit(solution)/shard_map/odd_t3/ppermute | solution.py:304
  37.6 4.2 %shard_map.37 = (f32[1024,8192]{1,0:T(8,128)}, f32[8,128]{1,0:T(8,128)S(1)}) custom-call(bf16[1024,768]{1,0:T(8,128)(2,1)S(1)} %get-tuple-element.42.refs_0_, f32[512,256]{1,0:T(8,128)S(1)} %get-tuple-element.51.refs_1_, f32[512,256]{1,0:T(8,128)S(1)} %get-tuple-element.55.refs_2_, f32[512,256]{1,0:T(8,128)S(1)} %collective-permute-done.8.refs_3_, ...), custom_call_target="tpu_custom_call" | custom-call | flops 10000000000 | bytes 100000000 | tf_op jit(solution)/shard_map/pallas_call | solution.py:247
  41.9 0.8 shard_map.38
  42.7 2.0 %collective-permute-start.13 = (f32[8,128]{1,0:T(8,128)S(1)}, f32[8,128]{1,0:T(8,128)S(1)}, u32[]{:S(2)}, u32[]{:S(2)}) collective-permute-start(f32[8,128]{1,0:T(8,128)S(1)} %get-tuple-element.59.token.refs_0_), channel_id=1, source_target_pairs={{0,8},{1,9},{2,10},{3,11},{4,12},{5,13},{6,14},{7,15},{8,0},{9,1},... | collective-permute-start | bytes 12296 | tf_op jit(solution)/shard_map/total_1/ppermute | solution.py:304
  44.7 0.3 collective-permute-start.15
  45.0 0.5 collective-permute-start.18
  45.6 0.1 shard_map.41
  45.7 1.0 %collective-permute-start.17 = (f32[512,256]{1,0:T(8,128)S(1)}, f32[512,256]{1,0:T(8,128)S(1)}, u32[]{:S(2)}, u32[]{:S(2)}) collective-permute-start(f32[512,256]{1,0:T(8,128)S(1)} %get-tuple-element.65.refs_2_), channel_id=1, source_target_pairs={{0,2},{1,5},{2,0},{3,7},{4,6},{5,1},{6,4},{7,3},{8,10},{9,13},{10,... | collective-permute-start | bytes 1572872 | tf_op jit(solution)/shard_map/odd_b2/ppermute | solution.py:304
  46.7 0.4 collective-permute-done.14.refs_0_
  47.1 0.7 shard_map.43
  47.8 4.2 %shard_map.44 = (f32[1024,8192]{1,0:T(8,128)}, f32[8,128]{1,0:T(8,128)S(1)}) custom-call(bf16[1024,768]{1,0:T(8,128)(2,1)S(1)} %get-tuple-element.42.refs_0_, f32[512,256]{1,0:T(8,128)S(1)} %get-tuple-element.64.refs_1_, f32[512,256]{1,0:T(8,128)S(1)} %get-tuple-element.65.refs_2_, ...), custom_call_target="tpu_custom_call", output_to_operand_aliasing={{0}: (4, {})} | custom-call | flops 10000000000 | bytes 100000000 | tf_op jit(solution)/shard_map/pallas_call | solution.py:247
  52.0 4.2 %collective-permute-done.15.refs_0_ = f32[512,256]{1,0:T(8,128)S(1)} collective-permute-done((f32[512,256]{1,0:T(8,128)S(1)}, f32[512,256]{1,0:T(8,128)S(1)}, u32[]{:S(2)}, u32[]{:S(2)}) %collective-permute-start.15) | collective-permute-done | bytes 524320 | tf_op jit(solution)/shard_map/far1/ppermute | solution.py:304
  56.3 0.1 shard_map.49
  56.4 0.7 collective-permute-start.21
  57.1 7.5 %collective-permute-start.11 = (f32[512,256]{1,0:T(8,128)S(1)}, f32[512,256]{1,0:T(8,128)S(1)}, u32[]{:S(2)}, u32[]{:S(2)}) collective-permute-start(f32[512,256]{1,0:T(8,128)S(1)} %shard_map.39.refs_2_), channel_id=1, source_target_pairs={{0,1},{1,0},{2,3},{3,2},{4,5},{5,4},{6,7},{7,6},{8,9},{9,8},{10,11... | collective-permute-start | bytes 1572872 | tf_op jit(solution)/shard_map/far_o/ppermute | solution.py:304
  64.7 1.7 %collective-permute-done.17.refs_0_ = f32[512,256]{1,0:T(8,128)S(1)} collective-permute-done((f32[512,256]{1,0:T(8,128)S(1)}, f32[512,256]{1,0:T(8,128)S(1)}, u32[]{:S(2)}, u32[]{:S(2)}) %collective-permute-start.17) | collective-permute-done | bytes 524320 | tf_op jit(solution)/shard_map/odd_b2/ppermute | solution.py:304
  66.5 0.7 shard_map.47
  67.2 0.4 collective-permute-start.20
  67.6 2.9 %collective-permute-done.20.refs_13_ = f32[8,128]{1,0:T(8,128)S(1)} collective-permute-done((f32[8,128]{1,0:T(8,128)S(1)}, f32[8,128]{1,0:T(8,128)S(1)}, u32[]{:S(2)}, u32[]{:S(2)}) %collective-permute-start.20) | collective-permute-done | bytes 4128 | tf_op jit(solution)/shard_map/total_2/ppermute | solution.py:304
  70.5 8.8 %shard_map.48 = (f32[1024,8192]{1,0:T(8,128)}, f32[8,128]{1,0:T(8,128)S(1)}) custom-call(bf16[1024,768]{1,0:T(8,128)(2,1)S(1)} %get-tuple-element.42.refs_0_, f32[512,256]{1,0:T(8,128)S(1)} %get-tuple-element.46.refs_1_, f32[512,256]{1,0:T(8,128)S(1)} %shard_map.39.refs_2_, ...), custom_call_target="tpu_custom_call", output_to_operand_aliasing={{0}: (11, {})} | custom-call | flops 1 | bytes 1 | tf_op jit(solution)/shard_map/pallas_call | solution.py:247
  79.4 0.7 shard_map.50
  80.1 1.7 %collective-permute-start.22 = (f32[1024,256]{1,0:T(8,128)S(1)}, f32[1024,256]{1,0:T(8,128)S(1)}, u32[]{:S(2)}, u32[]{:S(2)}) collective-permute-start(f32[1024,256]{1,0:T(8,128)S(1)} %get-tuple-element.78.refs_1_), channel_id=1, source_target_pairs={{0,1},{1,0},{2,3},{3,2},{4,5},{5,4},{6,7},{7,6},{8,9},{9,8},{10,11... | collective-permute-start | bytes 3145736 | tf_op jit(solution)/shard_map/last_o/ppermute | solution.py:304
  81.8 0.6 shard_map.53
  82.3 3.7 %shard_map.51 = (f32[1024,8192]{1,0:T(8,128)}, f32[8,128]{1,0:T(8,128)}) custom-call(bf16[1024,768]{1,0:T(8,128)(2,1)S(1)} %get-tuple-element.42.refs_0_, f32[1024,256]{1,0:T(8,128)S(1)} %get-tuple-element.78.refs_1_, f32[3072,256]{1,0:T(8,128)S(1)} %get-tuple-element.58.refs_5_.refs_2_.refs_1_, ...), custom_call_target="tpu_custom_call", output_to_operand_aliasing={{0}: (3, {})} | custom-call | flops 10000000000 | bytes 100000000 | tf_op jit(solution)/shard_map/pallas_call | solution.py:247
  86.0 2.6 %shard_map.52 = (f32[1024,8192]{1,0:T(8,128)}, f32[8,128]{1,0:T(8,128)}) custom-call(bf16[1024,768]{1,0:T(8,128)(2,1)S(1)} %get-tuple-element.42.refs_0_, f32[3072,256]{1,0:T(8,128)S(1)} %get-tuple-element.58.refs_5_.refs_2_.refs_1_, f32[1024,256]{1,0:T(8,128)S(1)} %collective-permute-done.22.refs_2_, ...), custom_call_target="tpu_custom_call", output_to_operand_aliasing={{0}: (3, {})} | custom-call | flops 10000000000 | bytes 100000000 | tf_op jit(solution)/shard_map/pallas_call | solution.py:247
  (23 shorter events, 0.3 us)
Async XLA Ops:
  1.7 2.8 %collective-permute-start = (f32[1024,128]{1,0:T(8,128)S(1)}, f32[1024,128]{1,0:T(8,128)S(1)}, u32[]{:S(2)}, u32[]{:S(2)}) collective-permute-start(f32[1024,128]{1,0:T(8,128)S(1)} %slice.3.mine), channel_id=1, source_target_pairs={{0,1},{1,0},{2,3},{3,2},{4,5},{5,4},{6,7},{7,6},{8,9},{9,8},{10,11... | collective-permute-start | bytes 1572872 | tf_op jit(solution)/shard_map/sib/ppermute | solution.py:304
  1.8 9.6 %collective-permute-start.1 = (f32[1024,128]{1,0:T(8,128)S(1)}, f32[1024,128]{1,0:T(8,128)S(1)}, u32[]{:S(2)}, u32[]{:S(2)}) collective-permute-start(f32[1024,128]{1,0:T(8,128)S(1)} %slice.3.mine), channel_id=1, source_target_pairs={{0,2},{1,5},{2,0},{3,7},{4,6},{5,1},{6,4},{7,3},{8,10},{9,13},{10,... | collective-permute-start | bytes 1572872 | tf_op jit(solution)/shard_map/raw1/ppermute | solution.py:304
  5.4 15.2 %collective-permute-start.2 = (f32[512,256]{1,0:T(8,128)S(1)}, f32[512,256]{1,0:T(8,128)S(1)}, u32[]{:S(2)}, u32[]{:S(2)}) collective-permute-start(f32[512,256]{1,0:T(8,128)S(1)} %get-tuple-element.46.refs_1_), channel_id=1, source_target_pairs={{0,24},{1,8},{2,26},{3,10},{4,28},{5,12},{6,30},{7,14},{8,0},{9,16... | collective-permute-start | bytes 1572872 | tf_op jit(solution)/shard_map/odd_t/ppermute | solution.py:304
  7.3 15.8 %collective-permute-start.3 = (f32[1024,128]{1,0:T(8,128)S(1)}, f32[1024,128]{1,0:T(8,128)S(1)}, u32[]{:S(2)}, u32[]{:S(2)}) collective-permute-start(f32[1024,128]{1,0:T(8,128)S(1)} %get-tuple-element.48), channel_id=1, source_target_pairs={{0,4},{1,3},{2,6},{3,1},{4,0},{5,7},{6,2},{7,5},{8,12},{9,11},{10,... | collective-permute-start | bytes 1572872 | tf_op jit(solution)/shard_map/raw2/ppermute | solution.py:304
  11.5 15.0 %collective-permute-start.4 = (f32[1024,128]{1,0:T(8,128)S(1)}, f32[1024,128]{1,0:T(8,128)S(1)}, u32[]{:S(2)}, u32[]{:S(2)}) collective-permute-start(f32[1024,128]{1,0:T(8,128)S(1)} %get-tuple-element.44.refs_0_), channel_id=1, source_target_pairs={{0,4},{1,3},{2,6},{3,1},{4,0},{5,7},{6,2},{7,5},{8,12},{9,11},{10,... | collective-permute-start | bytes 1572872 | tf_op jit(solution)/shard_map/raw3/ppermute | solution.py:304
  13.0 18.5 %collective-permute-start.6 = (f32[512,256]{1,0:T(8,128)S(1)}, f32[512,256]{1,0:T(8,128)S(1)}, u32[]{:S(2)}, u32[]{:S(2)}) collective-permute-start(f32[512,256]{1,0:T(8,128)S(1)} %get-tuple-element.53.refs_3_), channel_id=1, source_target_pairs={{0,24},{1,8},{2,26},{3,10},{4,28},{5,12},{6,30},{7,14},{8,0},{9,16... | collective-permute-start | bytes 1572872 | tf_op jit(solution)/shard_map/odd_b/ppermute | solution.py:304
  20.6 13.9 %collective-permute-start.7 = (f32[512,256]{1,0:T(8,128)S(1)}, f32[512,256]{1,0:T(8,128)S(1)}, u32[]{:S(2)}, u32[]{:S(2)}) collective-permute-start(f32[512,256]{1,0:T(8,128)S(1)} %get-tuple-element.51.refs_1_), channel_id=1, source_target_pairs={{0,2},{1,5},{2,0},{3,7},{4,6},{5,1},{6,4},{7,3},{8,10},{9,13},{10,... | collective-permute-start | bytes 1572872 | tf_op jit(solution)/shard_map/odd_t1/ppermute | solution.py:304
  21.9 14.4 %collective-permute-start.8 = (f32[512,256]{1,0:T(8,128)S(1)}, f32[512,256]{1,0:T(8,128)S(1)}, u32[]{:S(2)}, u32[]{:S(2)}) collective-permute-start(f32[512,256]{1,0:T(8,128)S(1)} %get-tuple-element.51.refs_1_), channel_id=1, source_target_pairs={{0,4},{1,3},{2,6},{3,1},{4,0},{5,7},{6,2},{7,5},{8,12},{9,11},{10,... | collective-permute-start | bytes 1572872 | tf_op jit(solution)/shard_map/odd_t2/ppermute | solution.py:304
  23.1 21.5 %collective-permute-start.9 = (f32[512,256]{1,0:T(8,128)S(1)}, f32[512,256]{1,0:T(8,128)S(1)}, u32[]{:S(2)}, u32[]{:S(2)}) collective-permute-start(f32[512,256]{1,0:T(8,128)S(1)} %get-tuple-element.51.refs_1_), channel_id=1, source_target_pairs={{1,9},{3,11},{5,13},{7,15},{8,16},{10,18},{12,20},{14,22},{16,24},... | collective-permute-start | bytes 1572872 | tf_op jit(solution)/shard_map/far_t/ppermute | solution.py:304
  31.6 13.1 %collective-permute-start.10 = (f32[512,256]{1,0:T(8,128)S(1)}, f32[512,256]{1,0:T(8,128)S(1)}, u32[]{:S(2)}, u32[]{:S(2)}) collective-permute-start(f32[512,256]{1,0:T(8,128)S(1)} %get-tuple-element.60.refs_0_), channel_id=1, source_target_pairs={{1,8},{3,10},{5,12},{7,14},{8,17},{10,19},{12,21},{14,23},{16,25},... | collective-permute-start | bytes 1572872 | tf_op jit(solution)/shard_map/far_b/ppermute | solution.py:304
  32.9 12.7 %collective-permute-start.12 = (f32[512,256]{1,0:T(8,128)S(1)}, f32[512,256]{1,0:T(8,128)S(1)}, u32[]{:S(2)}, u32[]{:S(2)}) collective-permute-start(f32[512,256]{1,0:T(8,128)S(1)} %get-tuple-element.60.refs_0_), channel_id=1, source_target_pairs={{0,4},{1,3},{2,6},{3,1},{4,0},{5,7},{6,2},{7,5},{8,12},{9,11},{10,... | collective-permute-start | bytes 1572872 | tf_op jit(solution)/shard_map/odd_b1/ppermute | solution.py:304
  34.5 7.3 %collective-permute-start.5 = (f32[3072,128]{1,0:T(8,128)S(1)}, f32[3072,128]{1,0:T(8,128)S(1)}, u32[]{:S(2)}, u32[]{:S(2)}) collective-permute-start(f32[3072,128]{1,0:T(8,128)S(1)} %shard_map.34.mine), channel_id=1, source_target_pairs={{0,1},{1,0},{2,3},{3,2},{4,5},{5,4},{6,7},{7,6},{8,9},{9,8},{10,11... | collective-permute-start | bytes 4718600 | tf_op jit(solution)/shard_map/other/ppermute | solution.py:304
  36.4 10.7 %collective-permute-start.14 = (f32[512,256]{1,0:T(8,128)S(1)}, f32[512,256]{1,0:T(8,128)S(1)}, u32[]{:S(2)}, u32[]{:S(2)}) collective-permute-start(f32[512,256]{1,0:T(8,128)S(1)} %get-tuple-element.55.refs_2_), channel_id=1, source_target_pairs={{0,4},{1,3},{2,6},{3,1},{4,0},{5,7},{6,2},{7,5},{8,12},{9,11},{10,... | collective-permute-start | bytes 1572872 | tf_op jit(solution)/shard_map/odd_t3/ppermute | solution.py:304
  42.7 4.0 %collective-permute-start.13 = (f32[8,128]{1,0:T(8,128)S(1)}, f32[8,128]{1,0:T(8,128)S(1)}, u32[]{:S(2)}, u32[]{:S(2)}) collective-permute-start(f32[8,128]{1,0:T(8,128)S(1)} %get-tuple-element.59.token.refs_0_), channel_id=1, source_target_pairs={{0,8},{1,9},{2,10},{3,11},{4,12},{5,13},{6,14},{7,15},{8,0},{9,1},... | collective-permute-start | bytes 12296 | tf_op jit(solution)/shard_map/total_1/ppermute | solution.py:304
  44.7 11.5 %collective-permute-start.15 = (f32[512,256]{1,0:T(8,128)S(1)}, f32[512,256]{1,0:T(8,128)S(1)}, u32[]{:S(2)}, u32[]{:S(2)}) collective-permute-start(f32[512,256]{1,0:T(8,128)S(1)} %shard_map.39.refs_2_), channel_id=1, source_target_pairs={{0,4},{1,3},{2,6},{3,1},{4,0},{5,7},{6,2},{7,5},{8,12},{9,11},{10,... | collective-permute-start | bytes 1572872 | tf_op jit(solution)/shard_map/far1/ppermute | solution.py:304
  45.0 21.5 %collective-permute-start.18 = (f32[512,256]{1,0:T(8,128)S(1)}, f32[512,256]{1,0:T(8,128)S(1)}, u32[]{:S(2)}, u32[]{:S(2)}) collective-permute-start(f32[512,256]{1,0:T(8,128)S(1)} %shard_map.39.refs_2_), channel_id=1, source_target_pairs={{0,2},{1,5},{2,0},{3,7},{4,6},{5,1},{6,4},{7,3},{8,10},{9,13},{10,... | collective-permute-start | bytes 1572872 | tf_op jit(solution)/shard_map/far2/ppermute | solution.py:304
  45.7 20.7 %collective-permute-start.17 = (f32[512,256]{1,0:T(8,128)S(1)}, f32[512,256]{1,0:T(8,128)S(1)}, u32[]{:S(2)}, u32[]{:S(2)}) collective-permute-start(f32[512,256]{1,0:T(8,128)S(1)} %get-tuple-element.65.refs_2_), channel_id=1, source_target_pairs={{0,2},{1,5},{2,0},{3,7},{4,6},{5,1},{6,4},{7,3},{8,10},{9,13},{10,... | collective-permute-start | bytes 1572872 | tf_op jit(solution)/shard_map/odd_b2/ppermute | solution.py:304
  56.4 23.0 %collective-permute-start.21 = (f32[1024,256]{1,0:T(8,128)S(1)}, f32[1024,256]{1,0:T(8,128)S(1)}, u32[]{:S(2)}, u32[]{:S(2)}) collective-permute-start(f32[1024,256]{1,0:T(8,128)S(1)} %shard_map.49), channel_id=1, source_target_pairs={{0,2},{1,5},{2,0},{3,7},{4,6},{5,1},{6,4},{7,3},{8,10},{9,13},{10,... | collective-permute-start | bytes 3145736 | tf_op jit(solution)/shard_map/last/ppermute | solution.py:304
  57.1 13.4 %collective-permute-start.11 = (f32[512,256]{1,0:T(8,128)S(1)}, f32[512,256]{1,0:T(8,128)S(1)}, u32[]{:S(2)}, u32[]{:S(2)}) collective-permute-start(f32[512,256]{1,0:T(8,128)S(1)} %shard_map.39.refs_2_), channel_id=1, source_target_pairs={{0,1},{1,0},{2,3},{3,2},{4,5},{5,4},{6,7},{7,6},{8,9},{9,8},{10,11... | collective-permute-start | bytes 1572872 | tf_op jit(solution)/shard_map/far_o/ppermute | solution.py:304
  64.7 5.9 %collective-permute-start.16 = (f32[512,256]{1,0:T(8,128)S(1)}, f32[512,256]{1,0:T(8,128)S(1)}, u32[]{:S(2)}, u32[]{:S(2)}) collective-permute-start(f32[512,256]{1,0:T(8,128)S(1)} %get-tuple-element.71.refs_6_.refs_0_), channel_id=1, source_target_pairs={{0,1},{1,0},{2,3},{3,2},{4,5},{5,4},{6,7},{7,6},{8,9},{9,8},{10,11... | collective-permute-start | bytes 1572872 | tf_op jit(solution)/shard_map/far1_o/ppermute | solution.py:304
  67.2 3.4 %collective-permute-start.19 = (f32[512,256]{1,0:T(8,128)S(1)}, f32[512,256]{1,0:T(8,128)S(1)}, u32[]{:S(2)}, u32[]{:S(2)}) collective-permute-start(f32[512,256]{1,0:T(8,128)S(1)} %get-tuple-element.74.refs_8_), channel_id=1, source_target_pairs={{0,1},{1,0},{2,3},{3,2},{4,5},{5,4},{6,7},{7,6},{8,9},{9,8},{10,11... | collective-permute-start | bytes 1572872 | tf_op jit(solution)/shard_map/far2_o/ppermute | solution.py:304
  67.2 3.4 %collective-permute-start.20 = (f32[8,128]{1,0:T(8,128)S(1)}, f32[8,128]{1,0:T(8,128)S(1)}, u32[]{:S(2)}, u32[]{:S(2)}) collective-permute-start(f32[8,128]{1,0:T(8,128)S(1)} %get-tuple-element.70.token.refs_12_), channel_id=1, source_target_pairs={{0,16},{1,17},{2,18},{3,19},{4,20},{5,21},{6,22},{7,23},{8,24},{9,... | collective-permute-start | bytes 12296 | tf_op jit(solution)/shard_map/total_2/ppermute | solution.py:304
  80.1 5.9 %collective-permute-start.22 = (f32[1024,256]{1,0:T(8,128)S(1)}, f32[1024,256]{1,0:T(8,128)S(1)}, u32[]{:S(2)}, u32[]{:S(2)}) collective-permute-start(f32[1024,256]{1,0:T(8,128)S(1)} %get-tuple-element.78.refs_1_), channel_id=1, source_target_pairs={{0,1},{1,0},{2,3},{3,2},{4,5},{5,4},{6,7},{7,6},{8,9},{9,8},{10,11... | collective-permute-start | bytes 3145736 | tf_op jit(solution)/shard_map/last_o/ppermute | solution.py:304
